TPU v7x, 32 devices: a whole 2x2x4 slice. The times are simulated.
32 devices in a mesh: ctx: 4 (over y, x), tp: 8 (over z, core).
Axes of the slice: x: 2, y: 2, z: 4, core: 2. Of those that a mesh axis runs over, the one named last changes fastest.
Arguments:
- query_rows: bfloat16 [4096, 4096], P('ctx', 'tp'), may hold values from -6 to 6
- key_rows: bfloat16 [4096, 4096], P('ctx', 'tp'), may hold values from -0.5 to 0.5
- value_rows: bfloat16 [4096, 4096], P('ctx', 'tp'), may hold values from -500 to 500
- gate_logits: bfloat16 [4096, 4096], P('ctx', 'tp'), may hold values from -6 to 6
- norm_gain: float32 [4096], P('tp'), may hold values from 0.1 to 1.9
- log_decay: float32 [32, 4096], P('tp', 'ctx'), may hold values from -3 to 0
- offsets: int32 [6], replicated, may hold values from 0 to 4095, as said below
- cotangent: bfloat16 [4096, 4096], P('ctx', 'tp'), may hold values from -6 to 6
Outputs:
- attended: bfloat16 [4096, 4096], P('ctx', 'tp')
- grad_query: bfloat16 [4096, 4096], P('ctx', 'tp')
- grad_key: bfloat16 [4096, 4096], P('ctx', 'tp')
- grad_value: bfloat16 [4096, 4096], P('ctx', 'tp')
- grad_gate: bfloat16 [4096, 4096], P('ctx', 'tp')
Inputs may be any that keep to these rules, and one draw needn't show every extreme that they name: offsets[0] is 0 and the entries rise strictly; each is the first token of a rollout; every entry after the first lies among the last 1024 tokens of the 4096.
All inputs are finite; a program needn't handle non-finite values.
Results may differ from a plain program's by a relative error of at most 0.0035.
Values sent between devices are 32-bit elements; how exact they have to be, the bound alone decides.
A program may use at most 128 MiB of HBM per device.

v0:
```python
import jax
import jax.numpy as jnp
from jax import lax
from jax.sharding import PartitionSpec as P

D_HEAD = 128
BLOCK = 512


EPS_NORM = 1e-06
HIGHEST = lax.Precision.HIGHEST


def prefix(value, axis, join, neutral, backward):
    count, mine = (lax.axis_size(axis), lax.axis_index(axis))
    pieces = jax.tree.map(lambda part: lax.all_gather(part, axis), value)
    if backward:
        pieces = jax.tree.map(lambda part: part[::-1], pieces)
        mine = count - 1 - mine
    subtotal = jax.tree.map(
        lambda part, zero: jnp.full_like(part, 0) + jnp.asarray(zero, part.dtype), value, neutral
    )

    def hop(position, subtotal):
        longer = join(subtotal, jax.tree.map(lambda part: part[position], pieces))
        return jax.tree.map(lambda new, old: jnp.where(position < mine, new, old), longer, subtotal)

    return lax.fori_loop(0, count - 1, hop, subtotal)


def segment_ids(offsets, positions):
    hits = (offsets[None, :] <= positions[:, None]).astype(jnp.int32)
    return jnp.sum(hits, axis=1) - 1


def block_tables(decay_block, segment_block, segment_before):
    running = jnp.cumsum(decay_block, axis=1)
    index_rows = jnp.arange(segment_block.shape[0])
    causal = (index_rows[None, :] <= index_rows[:, None]) & (
        segment_block[:, None] == segment_block[None, :]
    )
    within = jnp.where(
        causal[None], jnp.exp(jnp.minimum(running[:, :, None] - running[:, None, :], 0.0)), 0.0
    )
    carry_weight = jnp.where((segment_block == segment_before)[:, None], jnp.exp(running.T), 0.0)
    last_weight = jnp.where(
        (segment_block == segment_block[-1])[:, None],
        jnp.exp(jnp.minimum(running[:, -1:] - running, 0.0)).T,
        0.0,
    )
    factor = jnp.where(segment_block[-1] == segment_before, jnp.exp(running[:, -1]), 0.0)
    return (within, carry_weight, last_weight, factor)


def combine(earlier, later):
    return (earlier[0] * later[0], later[0][:, None, None] * earlier[1] + later[1])


def prefix_states(device_factor, summary):
    identity = (jnp.ones_like(device_factor), jnp.zeros_like(summary))
    return prefix((device_factor, summary), "ctx", combine, identity, False)[1]


def suffix_states(device_factor, summary):
    identity = (jnp.ones_like(device_factor), jnp.zeros_like(summary))
    return prefix((device_factor, summary), "ctx", combine, identity, True)[1]


def local(query_rows, key_rows, value_rows, gate_logits, norm_gain, log_decay, offsets, cotangent):
    head_count = log_decay.shape[0]
    local_tokens = query_rows.shape[0]
    block_count = local_tokens // BLOCK
    feature_total = lax.axis_size("tp") * query_rows.shape[1]
    first_token = lax.axis_index("ctx") * local_tokens
    positions = first_token + jnp.arange(local_tokens, dtype=jnp.int32)
    segments = segment_ids(offsets, positions)
    start_before = segment_ids(offsets, jnp.reshape(first_token - 1, (1,)))[0]
    layout = (local_tokens, head_count, D_HEAD)
    queries = query_rows.reshape(layout)
    key_heads = key_rows.reshape(layout)
    value_heads = value_rows.reshape(layout)
    tables = []
    weights_list = []
    inner_out = []
    local_states = []
    for block_index in range(block_count):
        block_start = block_index * BLOCK
        finish = block_start + BLOCK
        before = start_before if block_index == 0 else segments[block_start - 1]
        block_table = block_tables(
            log_decay[:, block_start:finish], segments[block_start:finish], before
        )
        scores = jnp.einsum(
            "thd,shd->hts",
            queries[block_start:finish],
            key_heads[block_start:finish],
            preferred_element_type=jnp.float32,
        )
        weights = (scores * block_table[0]).astype(jnp.bfloat16)
        inner_out.append(
            jnp.einsum(
                "hts,shd->thd",
                weights,
                value_heads[block_start:finish],
                preferred_element_type=jnp.float32,
            )
        )
        value_f = value_heads[block_start:finish].astype(jnp.float32)
        key_f = key_heads[block_start:finish].astype(jnp.float32)
        local_states.append(
            jnp.einsum(
                "shi,shj->hij", key_f * block_table[2][:, :, None], value_f, precision=HIGHEST
            )
        )
        tables.append(block_table)
        weights_list.append(weights)
    device_factor = tables[0][3]
    device_state = local_states[0]
    block_index = 1
    device_state = tables[block_index][3][:, None, None] * device_state + local_states[block_index]
    device_factor = device_factor * tables[block_index][3]
    carried = prefix_states(device_factor, device_state)
    state_before = []
    pieces = []
    for block_index in range(block_count):
        block_start = block_index * BLOCK
        finish = block_start + BLOCK
        state_before.append(carried)
        query_f = queries[block_start:finish].astype(jnp.float32)
        pieces.append(
            inner_out[block_index]
            + tables[block_index][1][:, :, None]
            * jnp.einsum("thi,hij->thj", query_f, carried, precision=HIGHEST)
        )
        carried = tables[block_index][3][:, None, None] * carried + local_states[block_index]
    attention = jnp.concatenate(pieces, axis=0)
    squares = lax.psum(jnp.sum(attention * attention, axis=(1, 2)), "tp")
    rms = jnp.sqrt(squares / feature_total + EPS_NORM)[:, None, None]
    normed = attention / rms
    gain_heads = norm_gain.reshape(1, head_count, D_HEAD)
    gate_sig = jax.nn.sigmoid(gate_logits.reshape(layout).astype(jnp.float32))
    attended = (normed * gain_heads * gate_sig).astype(jnp.bfloat16).reshape(local_tokens, -1)
    upstream = cotangent.reshape(layout).astype(jnp.float32)
    grad_gate = (
        (upstream * normed * gain_heads * gate_sig * (1.0 - gate_sig))
        .astype(jnp.bfloat16)
        .reshape(local_tokens, -1)
    )
    grad_normed = upstream * gain_heads * gate_sig
    inner = lax.psum(jnp.sum(grad_normed * normed, axis=(1, 2)), "tp")[:, None, None]
    grad_attn = (grad_normed - normed * (inner / feature_total)) / rms
    grad_low = grad_attn.astype(jnp.bfloat16)
    query_parts = []
    key_inner = []
    value_inner = []
    reverse_states = []
    for block_index in range(block_count):
        block_start = block_index * BLOCK
        finish = block_start + BLOCK
        grad_block = grad_attn[block_start:finish]
        low_block = grad_low[block_start:finish]
        back_scores = (
            jnp.einsum(
                "thd,shd->hts",
                low_block,
                value_heads[block_start:finish],
                preferred_element_type=jnp.float32,
            )
            * tables[block_index][0]
        ).astype(jnp.bfloat16)
        query_parts.append(
            jnp.einsum(
                "hts,shd->thd",
                back_scores,
                key_heads[block_start:finish],
                preferred_element_type=jnp.float32,
            )
            + tables[block_index][1][:, :, None]
            * jnp.einsum("thj,hij->thi", grad_block, state_before[block_index], precision=HIGHEST)
        )
        key_inner.append(
            jnp.einsum(
                "hts,thd->shd",
                back_scores,
                queries[block_start:finish],
                preferred_element_type=jnp.float32,
            )
        )
        value_inner.append(
            jnp.einsum(
                "hts,thd->shd",
                weights_list[block_index],
                low_block,
                preferred_element_type=jnp.float32,
            )
        )
        query_f = queries[block_start:finish].astype(jnp.float32)
        reverse_states.append(
            jnp.einsum(
                "thi,thj->hij",
                query_f * tables[block_index][1][:, :, None],
                grad_block,
                precision=HIGHEST,
            )
        )
    device_back = reverse_states[block_count - 1]
    block_index = 0
    device_back = tables[block_index][3][:, None, None] * device_back + reverse_states[block_index]
    coming = suffix_states(device_factor, device_back)
    key_parts = [None] * block_count
    value_parts = [None] * block_count
    for block_index in range(block_count - 1, -1, -1):
        block_start = block_index * BLOCK
        finish = block_start + BLOCK
        key_f = key_heads[block_start:finish].astype(jnp.float32)
        value_f = value_heads[block_start:finish].astype(jnp.float32)
        last_weight = tables[block_index][2][:, :, None]
        key_parts[block_index] = key_inner[block_index] + last_weight * jnp.einsum(
            "shj,hij->shi", value_f, coming, precision=HIGHEST
        )
        value_parts[block_index] = value_inner[block_index] + last_weight * jnp.einsum(
            "shi,hij->shj", key_f, coming, precision=HIGHEST
        )
        coming = tables[block_index][3][:, None, None] * coming + reverse_states[block_index]
    grad_query = jnp.concatenate(query_parts, axis=0).astype(jnp.bfloat16).reshape(local_tokens, -1)
    grad_key = jnp.concatenate(key_parts, axis=0).astype(jnp.bfloat16).reshape(local_tokens, -1)
    grad_value = jnp.concatenate(value_parts, axis=0).astype(jnp.bfloat16).reshape(local_tokens, -1)
    return (attended, grad_query, grad_key, grad_value, grad_gate)


def solution(mesh):
    placed = (
        P("ctx", "tp"),
        P("ctx", "tp"),
        P("ctx", "tp"),
        P("ctx", "tp"),
        P("tp"),
        P("tp", "ctx"),
        P(),
        P("ctx", "tp"),
    )
    return jax.shard_map(
        local,
        mesh=mesh,
        in_specs=placed,
        out_specs=(P("ctx", "tp"), P("ctx", "tp"), P("ctx", "tp"), P("ctx", "tp"), P("ctx", "tp")),
        check_vma=False,
    )
```

profile of v0, /device:TPU:0, one launch (start us, length us, event | category | flops | bytes accessed | tf_op | source)
XLA Modules:
  0.0 150.3 jit_solution(2368509075566751542)
XLA Ops:
  19.6 1.5 fusion.55
  24.0 1.4 convolution_add_fusion
  25.5 2.1 %fusion.53 = (bf16[512,512]{1,0:T(8,128)(2,1)S(1)}, bf16[512,512]{1,0:T(8,128)(2,1)}) fusion(bf16[1024,512]{1,0:T(8,128)(2,1)} %param.12), kind=kLoop, calls=%fused_computation.119 | loop fusion | bytes 2097152 | tf_op jit(solution)/shard_map/slice | solution.py:95
  27.5 11.4 %all-reduce = f32[16]{0:T(128)S(1)} all-reduce(f32[16]{0:T(128)S(1)} %get-tuple-element.293), channel_id=2, replica_groups=mesh['ctx'=4,'tp'=8] {'ctx'}, use_global_device_ids=true, to_apply=%add | all-reduce | flops 16 | bytes 128
  40.5 2.5 %copy.147 = bf16[1024,512]{0,1:T(8,128)(2,1)} copy(bf16[1024,512]{1,0:T(8,128)(2,1)} %param.19) | data formatting | bytes 2097152 | tf_op args[7]
  43.0 2.3 %copy.146 = bf16[1024,512]{0,1:T(8,128)(2,1)} copy(bf16[1024,512]{1,0:T(8,128)(2,1)} %param.15) | data formatting | bytes 2097152 | tf_op args[3]
  45.7 1.4 multiply_convert_fusion.3
  47.1 1.8 %convolution_bitcast_fusion.7 = f32[512,4,128]{0,2,1:T(8,128)} fusion(bf16[4,512,512]{2,1,0:T(8,128)(2,1)S(1)} %multiply_convert_fusion.3, bf16[512,4,128]{0,2,1:T(8,128)(2,1)S(1)} %bitcast.199), kind=kOutput, calls=%fused_computation.27 | convolution fusion | flops 268435456 | bytes 3670016 | tf_op jit(solution)/shard_map/hts,shd->thd/dot_general | solution.py:101
  48.9 1.4 multiply_convert_fusion.2
  50.4 1.3 copy-done.4
  51.7 1.8 %convolution_bitcast_fusion.6 = f32[512,4,128]{0,2,1:T(8,128)} fusion(bf16[4,512,512]{2,1,0:T(8,128)(2,1)S(1)} %multiply_convert_fusion.2, bf16[512,4,128]{0,2,1:T(8,128)(2,1)S(1)} %bitcast.207), kind=kOutput, calls=%fused_computation.26 | convolution fusion | flops 268435456 | bytes 3670016 | tf_op jit(solution)/shard_map/hts,shd->thd/dot_general | solution.py:101
  53.5 1.4 all-gather.6.cloned.1.call-done
  54.9 3.2 %while.28 = (s32[]{:T(128)}, f32[4,128,128]{2,1,0:T(8,128)S(1)}, s32[]{:T(128)}, f32[4,4]{1,0:T(4,128)S(1)}, f32[4,4,128,128]{3,2,1,0:T(8,128)}, /*index=5*/s32[]{:T(128)}, s32[]{:T(128)}) while((s32[]{:T(128)}, f32[4,128,128]{2,1,0:T(8,128)S(1)}, s32[]{:T(128)}, f32[4,4]{1,0:T(4,128)S(1)}, f32[4,4,128,128]{3,2,1,0:T(8,128)}, ...), condition=%wide.region_7.8_spmd.clone, body=%wide.region_6.7_spmd.clone.sunk | while | flops 262148 | bytes 786585 | solution.py:28
  58.2 2.0 %fusion.13 = f32[512,4,128]{0,2,1:T(8,128)S(1)} fusion(f32[512,4,128]{0,2,1:T(8,128)} %convolution_bitcast_fusion.7, f32[4,128,128]{2,1,0:T(8,128)S(1)} %get-tuple-element.193, bf16[512,4,128]{0,2,1:T(8,128)(2,1)S(1)} %bitcast.191, f32[512,4]{0,1:T(4,128)S(1)} %get-tuple-element.298), kind=kOutput, calls=%fused_computation.47 | convolution fusion | flops 403177472 | bytes 2891776 | tf_op jit(solution)/shard_map/thi,hij->thj/dot_general | solution.py:133
  61.1 16.4 %psum.14 = f32[1024]{0:T(1024)S(1)} all-reduce(f32[1024]{0:T(1024)S(1)} %multiply_reduce_fusion.1), channel_id=1, replica_groups=mesh['ctx'=4,'tp'=8] {'tp'}, use_global_device_ids=true, to_apply=%region_9.10 | all-reduce | flops 1024 | bytes 8192 | tf_op jit(solution)/shard_map/psum | solution.py:137
  77.5 4.3 %multiply_convert_fusion.4 = (bf16[1024,512]{0,1:T(8,128)(2,1)}, f32[1024]{0:T(1024)S(1)}, bf16[1024,512]{0,1:T(8,128)(2,1)}, f32[1024,512]{0,1:T(8,128)}) fusion(bf16[1024,512]{0,1:T(8,128)(2,1)} %copy.147, f32[512]{0:T(512)S(1)} %copy-done.35, f32[1024]{0:T(1024)S(1)} %add_sqrt_fusion, f32[512,512]{0,1:T(8,128)S(1)} %bitcast.187, ...), kind=kLoop, calls=%fused_computation.14 | loop fusion | flops 10484736 | bytes 8398848 | tf_op jit(solution)/shard_map/convert_element_type | solution.py:146
  81.8 13.6 %psum.15 = f32[1024]{0:T(1024)S(1)} all-reduce(f32[1024]{0:T(1024)S(1)} %get-tuple-element.269), channel_id=1, replica_groups=mesh['ctx'=4,'tp'=8] {'tp'}, use_global_device_ids=true, to_apply=%region_11.12 | all-reduce | flops 1024 | bytes 8192 | tf_op jit(solution)/shard_map/psum | solution.py:150
  95.4 3.1 %fusion.52 = (bf16[1024,4,128]{0,2,1:T(8,128)(2,1)S(1)}, f32[1024,4,128]{0,2,1:T(8,128)S(1)}) fusion(f32[1024]{0:T(1024)S(1)} %broadcast_multiply_fusion, f32[1024]{0:T(1024)S(1)} %add_sqrt_fusion, f32[512,4,128]{0,2,1:T(8,128)} %copy-done, f32[512,4,128]{0,2,1:T(8,128)} %copy-done.1, f32[1024,4,128]{0,2,1:T(8,128)} %bitcast.214, ...), kind=kLoop, calls=%fused_computation.118 | loop fusion | flops 4718592 | bytes 8398848 | tf_op jit(solution)/shard_map/convert_element_type | solution.py:152
  98.6 2.8 %multiply_convert_fusion.1 = bf16[4,512,512]{2,1,0:T(8,128)(2,1)} fusion(bf16[512,4,128]{0,2,1:T(8,128)(2,1)S(1)} %bitcast.200, f32[4,512]{1,0:T(4,128)S(1)} %bitcast.225, pred[512,512]{1,0:T(8,128)(4,1)S(1)} %copy-done.34, bf16[1024,4,128]{0,2,1:T(8,128)(2,1)S(1)} %get-tuple-element.266), kind=kOutput, calls=%fused_computation.7 | convolution fusion | flops 273678336 | bytes 3424256 | tf_op jit(solution)/shard_map/thd,shd->hts/dot_general | solution.py:163
  101.4 2.6 %multiply_convert_fusion = bf16[4,512,512]{2,1,0:T(8,128)(2,1)} fusion(bf16[512,4,128]{0,2,1:T(8,128)(2,1)S(1)} %bitcast.208, f32[4,512]{1,0:T(4,128)S(1)} %bitcast.228, pred[512,512]{1,0:T(8,128)(4,1)S(1)} %copy-done.32, bf16[1024,4,128]{0,2,1:T(8,128)(2,1)S(1)} %get-tuple-element.266), kind=kOutput, calls=%fused_computation.6 | convolution fusion | flops 273678336 | bytes 3424256 | tf_op jit(solution)/shard_map/thd,shd->hts/dot_general | solution.py:163
  105.1 1.9 %convolution_add_fusion.1 = f32[4,128,128]{2,1,0:T(8,128)} fusion(bf16[512,4,128]{0,2,1:T(8,128)(2,1)S(1)} %bitcast.192, f32[1024,4,128]{0,2,1:T(8,128)S(1)} %get-tuple-element.267, f32[512,4]{0,1:T(4,128)S(1)} %get-tuple-element.298, f32[4,128,128]{2,1,0:T(8,128)S(1)} %fusion.26, f32[4]{0:T(128)S(1)} %get-tuple-element.292), kind=kOutput, calls=%fused_computation.59 | convolution fusion | flops 403308544 | bytes 2105856 | tf_op jit(solution)/shard_map/thi,thj->hij/dot_general | solution.py:199
  107.1 2.6 %convolution_bitcast_fusion.5 = f32[512,4,128]{0,2,1:T(8,128)S(1)} fusion(bf16[4,512,512]{2,1,0:T(8,128)(2,1)} %multiply_convert_fusion.1, bf16[512,4,128]{0,2,1:T(8,128)(2,1)} %bitcast.204), kind=kOutput, calls=%fused_computation.25 | convolution fusion | flops 268435456 | bytes 3670016 | tf_op jit(solution)/shard_map/hts,shd->thd/dot_general | solution.py:172
  114.3 2.4 %copy.162 = bf16[1024,512]{1,0:T(8,128)(2,1)} copy(bf16[1024,512]{0,1:T(8,128)(2,1)} %get-tuple-element.270) | data formatting | bytes 2097152
  116.7 2.3 %copy.166 = bf16[1024,512]{1,0:T(8,128)(2,1)} copy(bf16[1024,512]{0,1:T(8,128)(2,1)} %get-tuple-element.268) | data formatting | bytes 2097152
  119.0 2.6 %convolution_bitcast_fusion.3 = f32[512,4,128]{0,2,1:T(8,128)} fusion(bf16[4,512,512]{2,1,0:T(8,128)(2,1)S(1)} %copy-done.3, bf16[1024,4,128]{0,2,1:T(8,128)(2,1)} %copy-done.27), kind=kOutput, calls=%fused_computation.23 | convolution fusion | flops 268435456 | bytes 3670016 | tf_op jit(solution)/shard_map/hts,thd->shd/dot_general | solution.py:190
  121.6 1.4 convolution_bitcast_fusion.2
  123.6 1.4 convolution_bitcast_fusion.1
  126.1 5.0 %all-gather.8.cloned.1.call-done = f32[16,128,128]{2,1,0:T(8,128)} async-done(((f32[4,128,128]{2,1,0:T(8,128)}), f32[16,128,128]{2,1,0:T(8,128)}) %all-gather.8.cloned.1.call-update) | async-done | bytes 1048592 | tf_op jit(solution)/shard_map/all_gather | solution.py:16
  133.4 2.0 %fusion.20 = bf16[512,4,128]{0,2,1:T(8,128)(2,1)S(1)} fusion(f32[512,4,128]{0,2,1:T(8,128)} %convolution_bitcast_fusion.3, bf16[512,4,128]{0,2,1:T(8,128)(2,1)S(1)} %bitcast.205, f32[512,4]{0,1:T(4,128)S(1)} %get-tuple-element.297, f32[4,128,128]{2,1,0:T(8,128)S(1)} %fusion.26, f32[4,128,128]{2,1,0:T(8,128)S(1)} %get-tuple-element.194, ...), kind=kOutput, calls=%fused_computation.54 | convolution fusion | flops 403570688 | bytes 2629648 | tf_op jit(solution)/shard_map/shi,hij->shj/dot_general | solution.py:221
  137.2 2.3 %copy.165 = bf16[1024,512]{1,0:T(8,128)(2,1)} copy(bf16[1024,512]{0,1:T(8,128)(2,1)} %pad_maximum_fusion.3) | data formatting | bytes 2097152
  139.5 1.9 %fusion.18 = bf16[512,4,128]{0,2,1:T(8,128)(2,1)S(1)} fusion(f32[512,4,128]{0,2,1:T(8,128)} %convolution_bitcast_fusion.1, bf16[512,4,128]{0,2,1:T(8,128)(2,1)S(1)} %bitcast.201, f32[512,4]{0,1:T(4,128)S(1)} %get-tuple-element.297, f32[4,128,128]{2,1,0:T(8,128)S(1)} %fusion.26, f32[4,128,128]{2,1,0:T(8,128)S(1)} %get-tuple-element.194, ...), kind=kOutput, calls=%fused_computation.52 | convolution fusion | flops 403570688 | bytes 2629648 | tf_op jit(solution)/shard_map/shj,hij->shi/dot_general | solution.py:218
  142.1 1.3 copy.164
  (147 shorter events, 30.7 us)
Async XLA Ops:
  7.2 47.7 %all-gather.6.cloned.1.call-start = ((), (), s32[]{:S(2)}) async-start(), calls=%async_computation | async-start | bytes 1310720 | tf_op jit(solution)/shard_map/all_gather | solution.py:16
  19.6 26.1 %copy-start.16 = (bf16[512,512]{0,1:T(8,128)(2,1)}, bf16[512,512]{0,1:T(8,128)(2,1)S(1)}, u32[]{:S(2)}) copy-start(bf16[512,512]{0,1:T(8,128)(2,1)S(1)} %copy.192) | copy-start | bytes 1572868
  21.3 25.8 %copy-start.13 = (bf16[512,512]{0,1:T(8,128)(2,1)}, bf16[512,512]{0,1:T(8,128)(2,1)S(1)}, u32[]{:S(2)}) copy-start(bf16[512,512]{0,1:T(8,128)(2,1)S(1)} %copy.132) | copy-start | bytes 1572868
  21.6 3.9 %copy-start.21 = (bf16[512,512]{0,1:T(8,128)(2,1)}, bf16[512,512]{0,1:T(8,128)(2,1)S(1)}, u32[]{:S(2)}) copy-start(bf16[512,512]{0,1:T(8,128)(2,1)S(1)} %copy.195) | copy-start | bytes 1572868
  21.8 28.6 %copy-start.18 = (bf16[512,512]{0,1:T(8,128)(2,1)}, bf16[512,512]{0,1:T(8,128)(2,1)S(1)}, u32[]{:S(2)}) copy-start(bf16[512,512]{0,1:T(8,128)(2,1)S(1)} %copy.196) | copy-start | bytes 1572868
  23.9 36.3 %copy-start.29 = (f32[4,128,128]{2,1,0:T(8,128)}, f32[4,128,128]{2,1,0:T(8,128)S(1)}, u32[]{:S(2)}) copy-start(f32[4,128,128]{2,1,0:T(8,128)S(1)} %fusion.31) | copy-start | bytes 786436
  25.4 105.6 %all-gather.8.cloned.1.call-start = ((), (), s32[]{:S(2)}) async-start(), calls=%async_computation.1 | async-start | bytes 1310720 | tf_op jit(solution)/shard_map/all_gather | solution.py:16
  40.5 8.4 %copy-start.9 = (bf16[512,512]{0,1:T(8,128)(2,1)}, bf16[512,512]{0,1:T(8,128)(2,1)S(1)}, u32[]{:S(2)}) copy-start(bf16[512,512]{0,1:T(8,128)(2,1)S(1)} %copy.197) | copy-start | bytes 1572868
  45.7 3.3 %copy-start.31 = (pred[512,512]{1,0:T(8,128)(4,1)}, pred[512,512]{1,0:T(8,128)(4,1)S(1)}, u32[]{:S(2)}) copy-start(pred[512,512]{1,0:T(8,128)(4,1)S(1)} %get-tuple-element.295) | copy-start | bytes 786436
  47.1 3.2 %copy-start.2 = (bf16[4,512,512]{2,1,0:T(8,128)(2,1)}, bf16[4,512,512]{2,1,0:T(8,128)(2,1)S(1)}, u32[]{:S(2)}) copy-start(bf16[4,512,512]{2,1,0:T(8,128)(2,1)S(1)} %multiply_convert_fusion.3) | copy-start | bytes 6291460
  58.1 2.0 %copy-start.10 = (bf16[512,512]{0,1:T(8,128)(2,1)S(1)}, bf16[512,512]{0,1:T(8,128)(2,1)}, u32[]{:S(2)}) copy-start(bf16[512,512]{0,1:T(8,128)(2,1)} %copy-done.9) | copy-start | bytes 1572868
  58.2 2.0 %copy-start.26 = (f32[512,4,128]{0,2,1:T(8,128)S(1)}, f32[512,4,128]{0,2,1:T(8,128)}, u32[]{:S(2)}) copy-start(f32[512,4,128]{0,2,1:T(8,128)} %convolution_bitcast_fusion.6) | copy-start | bytes 3145732
  60.1 17.4 %copy-start.1 = (f32[512,4,128]{0,2,1:T(8,128)}, f32[512,4,128]{0,2,1:T(8,128)S(1)}, u32[]{:S(2)}) copy-start(f32[512,4,128]{0,2,1:T(8,128)S(1)} %fusion.13) | copy-start | bytes 3145732
  60.2 17.3 %copy-start.35 = (f32[512]{0:T(512)S(1)}, f32[512]{0:T(512)}, u32[]{:S(2)}) copy-start(f32[512]{0:T(512)} %param.16) | copy-start | bytes 6148
  60.9 20.8 %copy-start = (f32[512,4,128]{0,2,1:T(8,128)}, f32[512,4,128]{0,2,1:T(8,128)S(1)}, u32[]{:S(2)}) copy-start(f32[512,4,128]{0,2,1:T(8,128)S(1)} %fusion.11) | copy-start | bytes 3145732
  95.4 3.2 %copy-start.14 = (bf16[512,512]{0,1:T(8,128)(2,1)S(1)}, bf16[512,512]{0,1:T(8,128)(2,1)}, u32[]{:S(2)}) copy-start(bf16[512,512]{0,1:T(8,128)(2,1)} %copy-done.13) | copy-start | bytes 1572868
  95.4 3.2 %copy-start.34 = (pred[512,512]{1,0:T(8,128)(4,1)S(1)}, pred[512,512]{1,0:T(8,128)(4,1)}, u32[]{:S(2)}) copy-start(pred[512,512]{1,0:T(8,128)(4,1)} %copy-done.33) | copy-start | bytes 786436
  98.5 2.8 %copy-start.27 = (bf16[1024,4,128]{0,2,1:T(8,128)(2,1)}, bf16[1024,4,128]{0,2,1:T(8,128)(2,1)S(1)}, u32[]{:S(2)}) copy-start(bf16[1024,4,128]{0,2,1:T(8,128)(2,1)S(1)} %get-tuple-element.266) | copy-start | bytes 3145732
  98.6 2.8 %copy-start.19 = (bf16[512,512]{0,1:T(8,128)(2,1)S(1)}, bf16[512,512]{0,1:T(8,128)(2,1)}, u32[]{:S(2)}) copy-start(bf16[512,512]{0,1:T(8,128)(2,1)} %copy-done.18) | copy-start | bytes 1572868
  98.6 2.8 %copy-start.32 = (pred[512,512]{1,0:T(8,128)(4,1)S(1)}, pred[512,512]{1,0:T(8,128)(4,1)}, u32[]{:S(2)}) copy-start(pred[512,512]{1,0:T(8,128)(4,1)} %copy-done.31) | copy-start | bytes 786436
  101.3 2.6 %copy-start.11 = (bf16[512,512]{0,1:T(8,128)(2,1)S(1)}, bf16[512,512]{0,1:T(8,128)(2,1)}, u32[]{:S(2)}) copy-start(bf16[512,512]{0,1:T(8,128)(2,1)} %copy-done.9) | copy-start | bytes 1572868
  107.0 2.7 %copy-start.7 = (bf16[4,512,512]{2,1,0:T(8,128)(2,1)S(1)}, bf16[4,512,512]{2,1,0:T(8,128)(2,1)}, u32[]{:S(2)}) copy-start(bf16[4,512,512]{2,1,0:T(8,128)(2,1)} %multiply_convert_fusion) | copy-start | bytes 6291460
  107.1 2.7 %copy-start.23 = (bf16[512,512]{0,1:T(8,128)(2,1)S(1)}, bf16[512,512]{0,1:T(8,128)(2,1)}, u32[]{:S(2)}) copy-start(bf16[512,512]{0,1:T(8,128)(2,1)} %copy-done.21) | copy-start | bytes 1572868
  114.3 4.7 %copy-start.3 = (bf16[4,512,512]{2,1,0:T(8,128)(2,1)S(1)}, bf16[4,512,512]{2,1,0:T(8,128)(2,1)}, u32[]{:S(2)}) copy-start(bf16[4,512,512]{2,1,0:T(8,128)(2,1)} %copy-done.2) | copy-start | bytes 6291460
  119.0 2.6 %copy-start.5 = (bf16[4,512,512]{2,1,0:T(8,128)(2,1)S(1)}, bf16[4,512,512]{2,1,0:T(8,128)(2,1)}, u32[]{:S(2)}) copy-start(bf16[4,512,512]{2,1,0:T(8,128)(2,1)} %copy-done.4) | copy-start | bytes 6291460
  119.0 2.6 %copy-start.28 = (bf16[1024,4,128]{0,2,1:T(8,128)(2,1)S(1)}, bf16[1024,4,128]{0,2,1:T(8,128)(2,1)}, u32[]{:S(2)}) copy-start(bf16[1024,4,128]{0,2,1:T(8,128)(2,1)} %copy-done.27) | copy-start | bytes 3145732
  121.6 2.0 %copy-start.6 = (bf16[4,512,512]{2,1,0:T(8,128)(2,1)S(1)}, bf16[4,512,512]{2,1,0:T(8,128)(2,1)}, u32[]{:S(2)}) copy-start(bf16[4,512,512]{2,1,0:T(8,128)(2,1)} %multiply_convert_fusion.1) | copy-start | bytes 6291460
  123.6 2.0 %copy-start.12 = (bf16[512,512]{0,1:T(8,128)(2,1)S(1)}, bf16[512,512]{0,1:T(8,128)(2,1)}, u32[]{:S(2)}) copy-start(bf16[512,512]{0,1:T(8,128)(2,1)} %copy-done.9) | copy-start | bytes 1572868
  132.8 2.6 %copy-start.24 = (bf16[512,512]{0,1:T(8,128)(2,1)S(1)}, bf16[512,512]{0,1:T(8,128)(2,1)}, u32[]{:S(2)}) copy-start(bf16[512,512]{0,1:T(8,128)(2,1)} %copy-done.21) | copy-start | bytes 1572868
  132.8 2.6 %copy-start.25 = (f32[512,4,128]{0,2,1:T(8,128)S(1)}, f32[512,4,128]{0,2,1:T(8,128)}, u32[]{:S(2)}) copy-start(f32[512,4,128]{0,2,1:T(8,128)} %convolution_bitcast_fusion.2) | copy-start | bytes 3145732
  136.1 3.5 %copy-start.15 = (bf16[512,512]{0,1:T(8,128)(2,1)S(1)}, bf16[512,512]{0,1:T(8,128)(2,1)}, u32[]{:S(2)}) copy-start(bf16[512,512]{0,1:T(8,128)(2,1)} %copy-done.13) | copy-start | bytes 1572868
  137.2 4.2 %copy-start.20 = (bf16[512,512]{0,1:T(8,128)(2,1)S(1)}, bf16[512,512]{0,1:T(8,128)(2,1)}, u32[]{:S(2)}) copy-start(bf16[512,512]{0,1:T(8,128)(2,1)} %copy-done.18) | copy-start | bytes 1572868
  (7 other events, 9.3 us)
Sparse Core Ops, SparseCore 0:
  25.5 29.3 all-gather.5
  107.2 23.8 all-gather.7
where the time goes:
time: 151 us; the launch traced here: 150 us
  blocking collectives  41.4 us (27%)
  matrix products  36.1 us (24%)
  local copies, waits for them, and re-layouts  29 us (19%)
  other arithmetic  19.2 us (13%)
  between operations  17.9 us (12%)
  waiting for transfers between devices  6.41 us (4%)
    unnamed x92, local copies, waits for them, and re-layouts  20.8 us
    psum x1, blocking collectives, local(): squares = lax.psum(jnp.sum(attention * attention, axis=(1, 2)), 'tp')  16.4 us
    psum x1, blocking collectives, local(): lax.psum(jnp.sum(grad_normed * normed, axis=(1, 2)), 'tp')[:, None, None]  13.6 us
    unnamed x1, blocking collectives  11.4 us
    all_gather x2, waiting for transfers between devices, prefix(): pieces = jax.tree.map(lambda part: lax.all_gather(part, axis), value)  6.38 us
    dot_general x2, matrix products, local(): jnp.einsum('thd,shd->hts', low_block, value_heads[block_start:finish], pr...  5.36 us
    convert_element_type x1, other arithmetic, local(): grad_gate = (upstream * normed * gain_heads * gate_sig * (1.0 - gate_sig)...  4.26 us
    dot_general x2, matrix products, local(): jnp.einsum('hts,thd->shd', weights_list[block_index], low_block, preferre...  4.03 us
  transfers between devices with their start and end apart: 2, of which 2 were waited for; matrix products, arithmetic and copies ran while one was open for 22% of the time, Pallas kernels for 0%

commit v1 on v0

v1 whole, which is shorter than its diff:
```python
import functools

import jax
import jax.numpy as jnp
from jax import lax
from jax.experimental import pallas as pl
from jax.experimental.pallas import tpu as pltpu
from jax.sharding import PartitionSpec as P

D_HEAD = 128
BLOCK = 512
HALF = 256
LANES = 128
EPS_NORM = 1e-06
MASKED = -1000.0
MESH = pl.DeviceIdType.MESH
F32 = jnp.float32
BF16 = jnp.bfloat16


def split(value):
    high = value.astype(BF16)
    return high, (value - high.astype(F32)).astype(BF16)


def dot(left, right, dims):
    return lax.dot_general(left, right, (dims, ((), ())), preferred_element_type=F32)


def mm(left, right):
    return dot(left, right, ((1,), (0,)))


def mm_rt(left, right):
    return dot(left, right, ((1,), (1,)))


def mm_lt(left, right):
    return dot(left, right, ((0,), (0,)))


def times_state(rows, state):
    return mm(jnp.concatenate([rows, rows], axis=1), jnp.concatenate(split(state), axis=0))


def times_state_t(rows, state):
    return mm_rt(jnp.concatenate([rows, rows], axis=1), jnp.concatenate(split(state), axis=1))


def outer_state(rows, weighted):
    both = mm_lt(rows, jnp.concatenate(split(weighted), axis=1))
    return both[:, :D_HEAD] + both[:, D_HEAD:]


def kernel(
    ctx_count, tp_count, heads, blocks,
    offs, q_ref, k_ref, v_ref, gate_ref, gain_ref, decay_ref, cot_ref,
    att_ref, dq_ref, dk_ref, dv_ref, dg_ref,
    run_row, run_col, carry, last, factor, bias, within, weights,
    attn, sig, gattn, key_acc, value_acc, states, local_state, back_state,
    total, prefix, send_state, recv_state, sums, recv_sums, scale_col,
    send_sem, recv_sem, sum_send_sem, sum_recv_sem,
):
    ctx = lax.axis_index("ctx")
    tp = lax.axis_index("tp")
    steps = (ctx_count - 1).bit_length()
    features = tp_count * heads * D_HEAD
    offset_count = offs.shape[0]

    def partner(step):
        size = 1 << step
        return ctx + size * (1 - 2 * ((ctx // size) % 2))

    def peer(hop):
        return lax.rem(tp + hop, tp_count)

    barrier = pltpu.get_barrier_semaphore()
    for step in range(steps):
        pl.semaphore_signal(barrier, inc=1, device_id=(partner(step), tp), device_id_type=MESH)
    for hop in range(1, tp_count):
        pl.semaphore_signal(barrier, inc=1, device_id=(ctx, peer(hop)), device_id_type=MESH)

    first = ctx * (blocks * BLOCK)

    def segment(positions):
        count = (offs[0] <= positions).astype(jnp.int32)
        for entry in range(1, offset_count):
            count = count + (offs[entry] <= positions).astype(jnp.int32)
        return count

    decays = jnp.concatenate(
        [decay_ref[:, b * BLOCK:(b + 1) * BLOCK] for b in range(blocks)], axis=0
    )
    rest = decays
    pieces = []
    for _ in range(3):
        piece = rest.astype(BF16)
        pieces.append(piece)
        rest = rest - piece.astype(F32)
    lower = lax.broadcasted_iota(jnp.int32, (BLOCK, BLOCK), 0)
    upper = lax.broadcasted_iota(jnp.int32, (BLOCK, BLOCK), 1)
    summing = jnp.where(lower <= upper, 1.0, 0.0).astype(BF16)
    running = mm(pieces[2], summing) + mm(pieces[1], summing) + mm(pieces[0], summing)
    run_row[...] = running
    lane = lax.broadcasted_iota(jnp.int32, (1, BLOCK), 1)
    sub = lax.broadcasted_iota(jnp.int32, (BLOCK, 1), 0)
    carry_rows, last_rows = [], []
    for b in range(blocks):
        start = first + b * BLOCK
        rows = running[b * heads:(b + 1) * heads]
        seg_row = segment(start + lane)
        seg_col = segment(start + sub)
        before = segment(start - 1)
        final = segment(start + BLOCK - 1)
        bias[b] = jnp.where((seg_col == seg_row) & (lower >= upper), 0.0, MASKED)
        carry_rows.append(jnp.where(seg_row == before, jnp.exp(rows), 0.0))
        end = rows[:, BLOCK - 1:]
        last_rows.append(jnp.where(seg_row == final, jnp.exp(jnp.minimum(end - rows, 0.0)), 0.0))
        whole = jnp.where(before == final, jnp.exp(end), 0.0)
        factor[b * heads:(b + 1) * heads, :] = jnp.broadcast_to(whole, (heads, LANES))
    count = heads * blocks
    stacked = jnp.concatenate(
        [running] + carry_rows + last_rows + [jnp.zeros((LANES - 3 * count, BLOCK), F32)], axis=0
    )
    columns = stacked.T
    for r in range(count):
        run_col[r] = jnp.broadcast_to(columns[:, r:r + 1], (BLOCK, LANES))
        carry[r] = jnp.broadcast_to(columns[:, count + r:count + r + 1], (BLOCK, LANES))
        last[r] = jnp.broadcast_to(columns[:, 2 * count + r:2 * count + r + 1], (BLOCK, LANES))

    def head_cols(h):
        return pl.ds(pl.multiple_of(h * D_HEAD, D_HEAD), D_HEAD)

    def block_rows(b):
        return pl.ds(b * BLOCK, BLOCK)

    def factor_of(b, h):
        return factor[pl.ds(b * heads + h, 1), :]

    def summarize(h, _):
        cols = head_cols(h)
        acc = None
        prod = None
        for b in range(blocks):
            r = b * heads + h
            weighted = v_ref[block_rows(b), cols].astype(F32) * last[r]
            state = outer_state(k_ref[block_rows(b), cols], weighted)
            local_state[r] = state
            fac = factor_of(b, h)
            acc = state if acc is None else fac * acc + state
            prod = fac if prod is None else prod * fac
        total[h, :D_HEAD, :] = acc
        total[h, D_HEAD:, :] = jnp.broadcast_to(prod, (8, LANES))
        return 0

    lax.fori_loop(0, heads, summarize, 0)
    pl.semaphore_wait(barrier, steps + tp_count - 1)

    def exchange(way, step, h):
        return pltpu.make_async_remote_copy(
            src_ref=send_state.at[way, step, h],
            dst_ref=recv_state.at[way, step, h],
            send_sem=send_sem.at[way, step, h],
            recv_sem=recv_sem.at[way, step, h],
            device_id=(partner(step), tp),
            device_id_type=MESH,
        )

    def begin(way):
        for h in range(heads):
            prefix[h, :D_HEAD, :] = jnp.zeros((D_HEAD, LANES), F32)
            prefix[h, D_HEAD:, :] = jnp.ones((8, LANES), F32)
            send_state[way, 0, h] = total[h]
            exchange(way, 0, h).start()

    def advance(way, step, h):
        exchange(way, step, h).wait()
        size = 1 << step
        bit = (ctx // size) % 2
        after = bit == 1 if way == 0 else bit == 0
        other = recv_state[way, step, h, :D_HEAD, :]
        other_factor = recv_state[way, step, h, D_HEAD:, :][:1]
        mine = total[h, :D_HEAD, :]
        my_factor = total[h, D_HEAD:, :][:1]
        so_far = prefix[h, :D_HEAD, :]
        so_far_factor = prefix[h, D_HEAD:, :][:1]
        prefix[h, :D_HEAD, :] = jnp.where(after, so_far_factor * other + so_far, so_far)
        prefix[h, D_HEAD:, :] = jnp.broadcast_to(
            jnp.where(after, so_far_factor * other_factor, so_far_factor), (8, LANES)
        )
        if step + 1 < steps:
            joined = jnp.where(after, my_factor * other + mine, other_factor * mine + other)
            total[h, :D_HEAD, :] = joined
            total[h, D_HEAD:, :] = jnp.broadcast_to(my_factor * other_factor, (8, LANES))
            send_state[way, step + 1, h] = total[h]
            exchange(way, step + 1, h).start()

    begin(0)

    def attend(h, _):
        cols = head_cols(h)
        for b in range(blocks):
            r = b * heads + h
            rows = block_rows(b)
            query, key, value = q_ref[rows, cols], k_ref[rows, cols], v_ref[rows, cols]
            for top, bottom in ((0, HALF), (HALF, BLOCK)):
                col = run_col[r, top:bottom, :]
                col = jnp.concatenate([col] * (bottom // LANES), axis=1)
                row = run_row[pl.ds(r, 1), :][:, :bottom]
                decay = jnp.exp(jnp.minimum(col - row, bias[b, top:bottom, :bottom]))
                within[r, top:bottom, :bottom] = decay
                scores = mm_rt(query[top:bottom], key[:bottom])
                weight = (scores * decay).astype(BF16)
                weights[r, top:bottom, :bottom] = weight
                attn[r, top:bottom, :] = mm(weight, value[:bottom])
            sig[r] = jax.nn.sigmoid(gate_ref[rows, cols].astype(F32))
        return 0

    lax.fori_loop(0, heads, attend, 0)
    for step in range(steps):
        for h in range(heads):
            advance(0, step, h)

    def sum_copy(b, hop):
        return pltpu.make_async_remote_copy(
            src_ref=sums.at[b],
            dst_ref=recv_sums.at[b, hop - 1],
            send_sem=sum_send_sem.at[b, hop - 1],
            recv_sem=sum_recv_sem.at[b, hop - 1],
            device_id=(ctx, peer(hop)),
            device_id_type=MESH,
        )

    def upstream(rows, cols, r):
        return cot_ref[rows, cols].astype(F32) * (gain_ref[:, cols] * sig[r])

    ones = jnp.ones((8, 2 * LANES), BF16)
    chunks = BLOCK // LANES
    for b in range(blocks):
        rows = block_rows(b)

        def carry_in(h, acc, b=b, rows=rows):
            cols = head_cols(h)
            r = b * heads + h
            state = prefix[h, :D_HEAD, :]
            states[r] = state
            value = attn[r] + carry[r] * times_state(q_ref[rows, cols], state)
            attn[r] = value
            prefix[h, :D_HEAD, :] = factor_of(b, h) * state + local_state[r]
            return acc[0] + value * value, acc[1] + upstream(rows, cols, r) * value

        zero = jnp.zeros((BLOCK, LANES), F32)
        squares, inners = lax.fori_loop(0, heads, carry_in, (zero, zero))
        for at, part in ((0, squares), (chunks, inners)):
            line = mm_rt(ones, jnp.concatenate(split(part), axis=1))
            for c in range(chunks):
                sums[b, at + c:at + c + 1, :] = line[:1, c * LANES:(c + 1) * LANES]
        for hop in range(1, tp_count):
            sum_copy(b, hop).start()

    for b in range(blocks):
        rows = block_rows(b)
        added = sums[b]
        for hop in range(1, tp_count):
            sum_copy(b, hop).wait()
            added = added + recv_sums[b, hop - 1]
        inverse = 1.0 / jnp.sqrt(added[:chunks] / features + EPS_NORM)
        mean_inner = added[chunks:] * inverse / features
        turned = jnp.concatenate(
            [inverse, mean_inner, jnp.zeros((LANES - 2 * chunks, LANES), F32)], axis=0
        ).T
        for c in range(chunks):
            here = pl.ds(c * LANES, LANES)
            scale_col[b, 0, here, :] = jnp.broadcast_to(turned[:, c:c + 1], (LANES, LANES))
            scale_col[b, 1, here, :] = jnp.broadcast_to(
                turned[:, chunks + c:chunks + c + 1], (LANES, LANES)
            )

        def grad_in(h, _, b=b, rows=rows):
            cols = head_cols(h)
            r = b * heads + h
            inv = scale_col[b, 0]
            grad = (upstream(rows, cols, r) - attn[r] * inv * scale_col[b, 1]) * inv
            gattn[r] = grad
            back_state[r] = outer_state(q_ref[rows, cols], grad * carry[r])
            return 0

        lax.fori_loop(0, heads, grad_in, 0)

    def summarize_back(h, _):
        acc = None
        prod = None
        for b in range(blocks - 1, -1, -1):
            r = b * heads + h
            fac = factor_of(b, h)
            acc = back_state[r] if acc is None else fac * acc + back_state[r]
            prod = fac if prod is None else prod * fac
        total[h, :D_HEAD, :] = acc
        total[h, D_HEAD:, :] = jnp.broadcast_to(prod, (8, LANES))
        return 0

    lax.fori_loop(0, heads, summarize_back, 0)
    begin(1)

    def retreat(h, _):
        cols = head_cols(h)
        for b in range(blocks):
            r = b * heads + h
            rows = block_rows(b)
            query, key, value = q_ref[rows, cols], k_ref[rows, cols], v_ref[rows, cols]
            normed = attn[r] * scale_col[b, 0]
            gate = sig[r]
            gated = normed * (gain_ref[:, cols] * gate)
            att_ref[rows, cols] = gated.astype(BF16)
            dg_ref[rows, cols] = (cot_ref[rows, cols].astype(F32) * gated * (1.0 - gate)).astype(BF16)
            high, low = split(gattn[r])
            state_high, state_low = split(states[r])
            crossed = mm_rt(
                jnp.concatenate([high, low], axis=1),
                jnp.concatenate([state_high, state_high], axis=1),
            ) + mm_rt(high, state_low)
            crossed = carry[r] * crossed
            back = []
            for top, bottom in ((0, HALF), (HALF, BLOCK)):
                scores = mm_rt(high[top:bottom], value[:bottom])
                piece = (scores * within[r, top:bottom, :bottom]).astype(BF16)
                back.append(piece)
                dq_ref[pl.ds(b * BLOCK + top, HALF), cols] = (
                    mm(piece, key[:bottom]) + crossed[top:bottom]
                ).astype(BF16)
            key_acc[r] = mm_lt(back[1], query[HALF:])
            key_acc[r, :HALF, :] += mm_lt(back[0], query[:HALF])
            value_acc[r] = mm_lt(weights[r, HALF:, :], high[HALF:])
            value_acc[r, :HALF, :] += mm_lt(weights[r, :HALF, :HALF], high[:HALF])
        return 0

    lax.fori_loop(0, heads, retreat, 0)
    for step in range(steps):
        for h in range(heads):
            advance(1, step, h)

    def finish(h, _):
        cols = head_cols(h)
        coming = prefix[h, :D_HEAD, :]
        for b in range(blocks - 1, -1, -1):
            r = b * heads + h
            rows = block_rows(b)
            dk_ref[rows, cols] = (
                key_acc[r] + last[r] * times_state_t(v_ref[rows, cols], coming)
            ).astype(BF16)
            dv_ref[rows, cols] = (
                value_acc[r] + last[r] * times_state(k_ref[rows, cols], coming)
            ).astype(BF16)
            if b > 0:
                coming = factor_of(b, h) * coming + back_state[r]
        return 0

    lax.fori_loop(0, heads, finish, 0)


def local(ctx_count, tp_count, query_rows, key_rows, value_rows, gate_logits, norm_gain, log_decay,
          offsets, cotangent):
    heads = log_decay.shape[0]
    tokens, width = query_rows.shape
    blocks = tokens // BLOCK
    count = heads * blocks
    steps = (ctx_count - 1).bit_length()
    out = jax.ShapeDtypeStruct((tokens, width), BF16)
    vmem = pl.BlockSpec(memory_space=pltpu.VMEM)
    tile = (count, BLOCK, LANES)
    state = (count, D_HEAD, D_HEAD)
    message = (heads, D_HEAD + 8, LANES)
    return pl.pallas_call(
        functools.partial(kernel, ctx_count, tp_count, heads, blocks),
        out_shape=(out,) * 5,
        in_specs=[pl.BlockSpec(memory_space=pltpu.SMEM)] + [vmem] * 7,
        out_specs=(vmem,) * 5,
        scratch_shapes=[
            pltpu.VMEM((count, BLOCK), F32),
            pltpu.VMEM(tile, F32),
            pltpu.VMEM(tile, F32),
            pltpu.VMEM(tile, F32),
            pltpu.VMEM((count, LANES), F32),
            pltpu.VMEM((blocks, BLOCK, BLOCK), F32),
            pltpu.VMEM((count, BLOCK, BLOCK), F32),
            pltpu.VMEM((count, BLOCK, BLOCK), BF16),
            pltpu.VMEM(tile, F32),
            pltpu.VMEM(tile, F32),
            pltpu.VMEM(tile, F32),
            pltpu.VMEM(tile, F32),
            pltpu.VMEM(tile, F32),
            pltpu.VMEM(state, F32),
            pltpu.VMEM(state, F32),
            pltpu.VMEM(state, F32),
            pltpu.VMEM(message, F32),
            pltpu.VMEM(message, F32),
            pltpu.VMEM((2, steps) + message, F32),
            pltpu.VMEM((2, steps) + message, F32),
            pltpu.VMEM((blocks, 8, LANES), F32),
            pltpu.VMEM((blocks, tp_count - 1, 8, LANES), F32),
            pltpu.VMEM((blocks, 2, BLOCK, LANES), F32),
            pltpu.SemaphoreType.DMA((2, steps, heads)),
            pltpu.SemaphoreType.DMA((2, steps, heads)),
            pltpu.SemaphoreType.DMA((blocks, tp_count - 1)),
            pltpu.SemaphoreType.DMA((blocks, tp_count - 1)),
        ],
        compiler_params=pltpu.CompilerParams(
            collective_id=0, has_side_effects=True, vmem_limit_bytes=56 * 1024 * 1024
        ),
    )(
        offsets, query_rows, key_rows, value_rows, gate_logits,
        norm_gain.reshape(1, width), log_decay, cotangent,
    )


def solution(mesh):
    rows = P("ctx", "tp")
    return jax.shard_map(
        functools.partial(local, mesh.shape["ctx"], mesh.shape["tp"]),
        mesh=mesh,
        in_specs=(rows, rows, rows, rows, P("tp"), P("tp", "ctx"), P(), rows),
        out_specs=(rows,) * 5,
        check_vma=False,
    )
```

time: 151 us -> 57.8 us (0.38)
  Pallas kernels: 0 us -> 48.7 us
  blocking collectives: 41.4 us -> 0 us
  matrix products: 36.1 us -> 0 us
  local copies, waits for them, and re-layouts: 29 us -> 8.13 us
  other arithmetic: 19.2 us -> 0 us
  between operations: 17.9 us -> 0.66 us
  waiting for transfers between devices: 6.41 us -> 0 us
    pallas_call x0 -> x1, Pallas kernels: none -> 48.7 us  [local(): pl.pallas_call(functools.partial(kernel, ctx_count, tp_count, heads, bloc...]
    dot_general x24 -> x0, matrix products: 36.1 us -> none  [the longest x2 5.36 us: local(): jnp.einsum('thd,shd->hts', low_block, value_heads[block_start:finish], pr...]
    psum x2 -> x0, blocking collectives: 29.9 us -> none  [the longest x1 16.4 us: local(): squares = lax.psum(jnp.sum(attention * attention, axis=(1, 2)), 'tp')]
    unnamed x92 -> x13, local copies, waits for them, and re-layouts: 20.8 us -> 8.13 us
    unnamed x1 -> x0, blocking collectives: 11.4 us -> none
    convert_element_type x2 -> x0, other arithmetic: 7.38 us -> none  [the longest x1 4.26 us: local(): grad_gate = (upstream * normed * gain_heads * gate_sig * (1.0 - gate_sig)...]
    slice x10 -> x0, local copies, waits for them, and re-layouts: 6.62 us -> none  [the longest x1 2.06 us: local(): queries[block_start:finish]]
    all_gather x2 -> x0, waiting for transfers between devices: 6.38 us -> none  [prefix(): pieces = jax.tree.map(lambda part: lax.all_gather(part, axis), value)]
  transfers between devices with their start and end apart: 2 -> 0, of which waited for: 2 -> 0; matrix products, arithmetic and copies ran while one was open for 22% -> 0% of each run, Pallas kernels for 0% -> 0%
where the time goes in v1:
time: 57.8 us; the launch traced here: 57.5 us
  Pallas kernels  48.7 us (84%)
  local copies, waits for them, and re-layouts  8.13 us (14%)
  between operations  0.66 us (1%)
    pallas_call x1, Pallas kernels, local(): pl.pallas_call(functools.partial(kernel, ctx_count, tp_count, heads, bloc...  48.7 us
    unnamed x13, local copies, waits for them, and re-layouts  8.13 us

profile of v1, /device:TPU:0, one launch (start us, length us, event | category | flops | bytes accessed | tf_op | source)
XLA Modules:
  0.0 57.5 jit_solution(4042243186218263294)
XLA Ops:
  0.6 48.7 %shard_map.119 = (bf16[1024,512]{1,0:T(8,128)(2,1)}, bf16[1024,512]{1,0:T(8,128)(2,1)}, bf16[1024,512]{1,0:T(8,128)(2,1)}, bf16[1024,512]{1,0:T(8,128)(2,1)}, bf16[1024,512]{1,0:T(8,128)(2,1)}) custom-call(s32[6]{0:T(128)} %offs.1, bf16[1024,512]{1,0:T(8,128)(2,1)} %q_ref.1, bf16[1024,512]{1,0:T(8,128)(2,1)} %k_ref.1, bf16[1024,512]{1,0:T(8,128)(2,1)} %v_ref.1, ...), custom_call_target="tpu_custom_call" | custom-call | tf_op jit(solution)/shard_map/pallas_call | solution.py:373
  49.4 0.0 copy-start.3
  49.4 2.4 %copy.18 = bf16[1024,512]{1,0:T(8,128)(2,1)} copy(bf16[1024,512]{1,0:T(8,128)(2,1)} %get-tuple-element.10) | data formatting | bytes 2097152
  51.7 0.0 copy-done.3
  51.7 0.0 copy-start.2
  51.7 1.0 %copy.19 = bf16[1024,512]{1,0:T(8,128)(2,1)} copy(bf16[1024,512]{1,0:T(8,128)(2,1)S(1)} %copy-done.3) | data formatting | bytes 2097152
  52.7 0.6 %copy-done.2 = bf16[1024,512]{1,0:T(8,128)(2,1)S(1)} copy-done((bf16[1024,512]{1,0:T(8,128)(2,1)S(1)}, bf16[1024,512]{1,0:T(8,128)(2,1)}, u32[]{:S(2)}) %copy-start.2) | copy-done | bytes 1048600
  53.3 0.0 copy-start.1
  53.3 1.0 %copy.20 = bf16[1024,512]{1,0:T(8,128)(2,1)} copy(bf16[1024,512]{1,0:T(8,128)(2,1)S(1)} %copy-done.2) | data formatting | bytes 2097152
  54.3 0.6 %copy-done.1 = bf16[1024,512]{1,0:T(8,128)(2,1)S(1)} copy-done((bf16[1024,512]{1,0:T(8,128)(2,1)S(1)}, bf16[1024,512]{1,0:T(8,128)(2,1)}, u32[]{:S(2)}) %copy-start.1) | copy-done | bytes 1048600
  54.9 0.0 copy-start
  54.9 1.0 %copy.21 = bf16[1024,512]{1,0:T(8,128)(2,1)} copy(bf16[1024,512]{1,0:T(8,128)(2,1)S(1)} %copy-done.1) | data formatting | bytes 2097152
  55.9 0.6 %copy-done = bf16[1024,512]{1,0:T(8,128)(2,1)S(1)} copy-done((bf16[1024,512]{1,0:T(8,128)(2,1)S(1)}, bf16[1024,512]{1,0:T(8,128)(2,1)}, u32[]{:S(2)}) %copy-start) | copy-done | bytes 1048600
  56.5 1.0 %copy.22 = bf16[1024,512]{1,0:T(8,128)(2,1)} copy(bf16[1024,512]{1,0:T(8,128)(2,1)S(1)} %copy-done) | data formatting | bytes 2097152
Async XLA Ops:
  49.4 2.4 %copy-start.3 = (bf16[1024,512]{1,0:T(8,128)(2,1)S(1)}, bf16[1024,512]{1,0:T(8,128)(2,1)}, u32[]{:S(2)}) copy-start(bf16[1024,512]{1,0:T(8,128)(2,1)} %get-tuple-element.11) | copy-start | bytes 3145732
  51.7 1.6 %copy-start.2 = (bf16[1024,512]{1,0:T(8,128)(2,1)S(1)}, bf16[1024,512]{1,0:T(8,128)(2,1)}, u32[]{:S(2)}) copy-start(bf16[1024,512]{1,0:T(8,128)(2,1)} %get-tuple-element.12) | copy-start | bytes 3145732
  53.3 1.6 %copy-start.1 = (bf16[1024,512]{1,0:T(8,128)(2,1)S(1)}, bf16[1024,512]{1,0:T(8,128)(2,1)}, u32[]{:S(2)}) copy-start(bf16[1024,512]{1,0:T(8,128)(2,1)} %get-tuple-element.13) | copy-start | bytes 3145732
  54.9 1.6 %copy-start = (bf16[1024,512]{1,0:T(8,128)(2,1)S(1)}, bf16[1024,512]{1,0:T(8,128)(2,1)}, u32[]{:S(2)}) copy-start(bf16[1024,512]{1,0:T(8,128)(2,1)} %get-tuple-element.14) | copy-start | bytes 3145732

commit v2 on v1

--- a/solution.py
+++ b/solution.py
@@ -54,13 +54,22 @@
 
 def kernel(
     ctx_count, tp_count, heads, blocks,
-    offs, q_ref, k_ref, v_ref, gate_ref, gain_ref, decay_ref, cot_ref,
-    att_ref, dq_ref, dk_ref, dv_ref, dg_ref,
-    run_row, run_col, carry, last, factor, bias, within, weights,
-    attn, sig, gattn, key_acc, value_acc, states, local_state, back_state,
-    total, prefix, send_state, recv_state, sums, recv_sums, scale_col,
-    send_sem, recv_sem, sum_send_sem, sum_recv_sem,
+    offs, q_hbm, k_hbm, v_hbm, gate_hbm, gain_ref, decay_ref, cot_hbm,
+    att_ref, dq_ref, dg_ref, key_acc, value_acc, last, factor, back_state, prefix,
+    run_row, run_col, carry, bias, within, weights,
+    attn, sig, gattn, states, local_state,
+    total, send_state, recv_state, sums, recv_sums, scale_col,
+    q_ref, k_ref, v_ref, gate_ref, cot_ref,
+    send_sem, recv_sem, sum_send_sem, sum_recv_sem, load_sem,
 ):
+    loads = [
+        pltpu.make_async_copy(src, dst, load_sem.at[i])
+        for i, (src, dst) in enumerate((
+            (k_hbm, k_ref), (v_hbm, v_ref), (q_hbm, q_ref), (gate_hbm, gate_ref), (cot_hbm, cot_ref),
+        ))
+    ]
+    for load in loads:
+        load.start()
     ctx = lax.axis_index("ctx")
     tp = lax.axis_index("tp")
     steps = (ctx_count - 1).bit_length()
@@ -137,25 +146,6 @@
     def factor_of(b, h):
         return factor[pl.ds(b * heads + h, 1), :]
 
-    def summarize(h, _):
-        cols = head_cols(h)
-        acc = None
-        prod = None
-        for b in range(blocks):
-            r = b * heads + h
-            weighted = v_ref[block_rows(b), cols].astype(F32) * last[r]
-            state = outer_state(k_ref[block_rows(b), cols], weighted)
-            local_state[r] = state
-            fac = factor_of(b, h)
-            acc = state if acc is None else fac * acc + state
-            prod = fac if prod is None else prod * fac
-        total[h, :D_HEAD, :] = acc
-        total[h, D_HEAD:, :] = jnp.broadcast_to(prod, (8, LANES))
-        return 0
-
-    lax.fori_loop(0, heads, summarize, 0)
-    pl.semaphore_wait(barrier, steps + tp_count - 1)
-
     def exchange(way, step, h):
         return pltpu.make_async_remote_copy(
             src_ref=send_state.at[way, step, h],
@@ -166,12 +156,15 @@
             device_id_type=MESH,
         )
 
-    def begin(way):
-        for h in range(heads):
-            prefix[h, :D_HEAD, :] = jnp.zeros((D_HEAD, LANES), F32)
-            prefix[h, D_HEAD:, :] = jnp.ones((8, LANES), F32)
-            send_state[way, 0, h] = total[h]
-            exchange(way, 0, h).start()
+    def begin(way, h, state, state_factor):
+        prefix[h, :D_HEAD, :] = jnp.zeros((D_HEAD, LANES), F32)
+        prefix[h, D_HEAD:, :] = jnp.ones((8, LANES), F32)
+        spread = jnp.broadcast_to(state_factor, (8, LANES))
+        total[h, :D_HEAD, :] = state
+        total[h, D_HEAD:, :] = spread
+        send_state[way, 0, h, :D_HEAD, :] = state
+        send_state[way, 0, h, D_HEAD:, :] = spread
+        exchange(way, 0, h).start()
 
     def advance(way, step, h):
         exchange(way, step, h).wait()
@@ -182,21 +175,49 @@
         other_factor = recv_state[way, step, h, D_HEAD:, :][:1]
         mine = total[h, :D_HEAD, :]
         my_factor = total[h, D_HEAD:, :][:1]
+        if step + 1 < steps:
+            joined = jnp.where(after, my_factor * other + mine, other_factor * mine + other)
+            spread = jnp.broadcast_to(my_factor * other_factor, (8, LANES))
+            send_state[way, step + 1, h, :D_HEAD, :] = joined
+            send_state[way, step + 1, h, D_HEAD:, :] = spread
+            exchange(way, step + 1, h).start()
+            total[h, :D_HEAD, :] = joined
+            total[h, D_HEAD:, :] = spread
         so_far = prefix[h, :D_HEAD, :]
         so_far_factor = prefix[h, D_HEAD:, :][:1]
         prefix[h, :D_HEAD, :] = jnp.where(after, so_far_factor * other + so_far, so_far)
         prefix[h, D_HEAD:, :] = jnp.broadcast_to(
             jnp.where(after, so_far_factor * other_factor, so_far_factor), (8, LANES)
         )
-        if step + 1 < steps:
-            joined = jnp.where(after, my_factor * other + mine, other_factor * mine + other)
-            total[h, :D_HEAD, :] = joined
-            total[h, D_HEAD:, :] = jnp.broadcast_to(my_factor * other_factor, (8, LANES))
-            send_state[way, step + 1, h] = total[h]
-            exchange(way, step + 1, h).start()
-
-    begin(0)
-
+
+    def advance_rest(way):
+        for step in range(1, steps - 1):
+            for h in range(heads):
+                advance(way, step, h)
+
+    pl.semaphore_wait(barrier, steps + tp_count - 1)
+    loads[0].wait()
+    loads[1].wait()
+
+    def summarize(h, _):
+        cols = head_cols(h)
+        acc = None
+        prod = None
+        for b in range(blocks):
+            r = b * heads + h
+            weighted = v_ref[block_rows(b), cols].astype(F32) * last[r]
+            state = outer_state(k_ref[block_rows(b), cols], weighted)
+            local_state[r] = state
+            fac = factor_of(b, h)
+            acc = state if acc is None else fac * acc + state
+            prod = fac if prod is None else prod * fac
+        begin(0, h, acc, prod)
+        return 0
+
+    lax.fori_loop(0, heads, summarize, 0)
+
+    loads[2].wait()
+    loads[3].wait()
     def attend(h, _):
         cols = head_cols(h)
         for b in range(blocks):
@@ -214,12 +235,13 @@
                 weights[r, top:bottom, :bottom] = weight
                 attn[r, top:bottom, :] = mm(weight, value[:bottom])
             sig[r] = jax.nn.sigmoid(gate_ref[rows, cols].astype(F32))
+        if steps > 1:
+            advance(0, 0, h)
         return 0
 
     lax.fori_loop(0, heads, attend, 0)
-    for step in range(steps):
-        for h in range(heads):
-            advance(0, step, h)
+    advance_rest(0)
+    loads[4].wait()
 
     def sum_copy(b, hop):
         return pltpu.make_async_remote_copy(
@@ -242,6 +264,8 @@
         def carry_in(h, acc, b=b, rows=rows):
             cols = head_cols(h)
             r = b * heads + h
+            if b == 0 and steps > 0:
+                advance(0, steps - 1, h)
             state = prefix[h, :D_HEAD, :]
             states[r] = state
             value = attn[r] + carry[r] * times_state(q_ref[rows, cols], state)
@@ -283,24 +307,16 @@
             grad = (upstream(rows, cols, r) - attn[r] * inv * scale_col[b, 1]) * inv
             gattn[r] = grad
             back_state[r] = outer_state(q_ref[rows, cols], grad * carry[r])
+            if b == blocks - 1:
+                acc = back_state[r]
+                prod = factor_of(b, h)
+                for e in range(blocks - 2, -1, -1):
+                    acc = factor_of(e, h) * acc + back_state[e * heads + h]
+                    prod = prod * factor_of(e, h)
+                begin(1, h, acc, prod)
             return 0
 
         lax.fori_loop(0, heads, grad_in, 0)
-
-    def summarize_back(h, _):
-        acc = None
-        prod = None
-        for b in range(blocks - 1, -1, -1):
-            r = b * heads + h
-            fac = factor_of(b, h)
-            acc = back_state[r] if acc is None else fac * acc + back_state[r]
-            prod = fac if prod is None else prod * fac
-        total[h, :D_HEAD, :] = acc
-        total[h, D_HEAD:, :] = jnp.broadcast_to(prod, (8, LANES))
-        return 0
-
-    lax.fori_loop(0, heads, summarize_back, 0)
-    begin(1)
 
     def retreat(h, _):
         cols = head_cols(h)
@@ -332,30 +348,54 @@
             key_acc[r, :HALF, :] += mm_lt(back[0], query[:HALF])
             value_acc[r] = mm_lt(weights[r, HALF:, :], high[HALF:])
             value_acc[r, :HALF, :] += mm_lt(weights[r, :HALF, :HALF], high[:HALF])
+        if steps > 1:
+            advance(1, 0, h)
         return 0
 
     lax.fori_loop(0, heads, retreat, 0)
-    for step in range(steps):
+    advance_rest(1)
+    if steps > 0:
         for h in range(heads):
-            advance(1, step, h)
-
-    def finish(h, _):
-        cols = head_cols(h)
-        coming = prefix[h, :D_HEAD, :]
-        for b in range(blocks - 1, -1, -1):
-            r = b * heads + h
-            rows = block_rows(b)
+            advance(1, steps - 1, h)
+
+
+def finish_kernel(
+    heads, blocks,
+    k_ref, v_ref, att_in, dq_in, dg_in, key_acc, value_acc, last, factor, back_state, prefix,
+    att_out, dq_out, dk_out, dv_out, dg_out,
+    dk_ref, dv_ref, coming_ref, ready_sem, block_sem,
+):
+    ready = [
+        pltpu.make_async_copy(src, dst, ready_sem.at[i])
+        for i, (src, dst) in enumerate(((att_in, att_out), (dq_in, dq_out), (dg_in, dg_out)))
+    ]
+    for copy in ready:
+        copy.start()
+    for h in range(heads):
+        coming_ref[h] = prefix[h, :D_HEAD, :]
+    for b in range(blocks - 1, -1, -1):
+        rows = pl.ds(b * BLOCK, BLOCK)
+
+        def finish(h, _, b=b, rows=rows):
+            cols = pl.ds(pl.multiple_of(h * D_HEAD, D_HEAD), D_HEAD)
+            r = b * heads + h
+            coming = coming_ref[h]
             dk_ref[rows, cols] = (
                 key_acc[r] + last[r] * times_state_t(v_ref[rows, cols], coming)
             ).astype(BF16)
             dv_ref[rows, cols] = (
                 value_acc[r] + last[r] * times_state(k_ref[rows, cols], coming)
             ).astype(BF16)
-            if b > 0:
-                coming = factor_of(b, h) * coming + back_state[r]
-        return 0
-
-    lax.fori_loop(0, heads, finish, 0)
+            coming_ref[h] = factor[pl.ds(r, 1), :] * coming + back_state[r]
+            return 0
+
+        lax.fori_loop(0, heads, finish, 0)
+        for i, (src, dst) in enumerate(((dk_ref, dk_out), (dv_ref, dv_out))):
+            copy = pltpu.make_async_copy(src.at[rows, :], dst.at[rows, :], block_sem.at[b, i])
+            copy.start()
+            ready.append(copy)
+    for copy in ready:
+        copy.wait()
 
 
 def local(ctx_count, tp_count, query_rows, key_rows, value_rows, gate_logits, norm_gain, log_decay,
@@ -367,50 +407,75 @@
     steps = (ctx_count - 1).bit_length()
     out = jax.ShapeDtypeStruct((tokens, width), BF16)
     vmem = pl.BlockSpec(memory_space=pltpu.VMEM)
+    anywhere = pl.BlockSpec(memory_space=pl.ANY)
     tile = (count, BLOCK, LANES)
     state = (count, D_HEAD, D_HEAD)
     message = (heads, D_HEAD + 8, LANES)
-    return pl.pallas_call(
+    held = pl.pallas_call(
         functools.partial(kernel, ctx_count, tp_count, heads, blocks),
-        out_shape=(out,) * 5,
-        in_specs=[pl.BlockSpec(memory_space=pltpu.SMEM)] + [vmem] * 7,
-        out_specs=(vmem,) * 5,
+        out_shape=(
+            pltpu.VMEM((tokens, width), BF16),
+            pltpu.VMEM((tokens, width), BF16),
+            pltpu.VMEM((tokens, width), BF16),
+            pltpu.VMEM(tile, F32),
+            pltpu.VMEM(tile, F32),
+            pltpu.VMEM(tile, F32),
+            pltpu.VMEM((count, LANES), F32),
+            pltpu.VMEM(state, F32),
+            pltpu.VMEM(message, F32),
+        ),
+        in_specs=[pl.BlockSpec(memory_space=pltpu.SMEM)] + [anywhere] * 4 + [vmem] * 2 + [anywhere],
+        out_specs=(vmem,) * 9,
         scratch_shapes=[
             pltpu.VMEM((count, BLOCK), F32),
             pltpu.VMEM(tile, F32),
             pltpu.VMEM(tile, F32),
-            pltpu.VMEM(tile, F32),
-            pltpu.VMEM((count, LANES), F32),
             pltpu.VMEM((blocks, BLOCK, BLOCK), F32),
             pltpu.VMEM((count, BLOCK, BLOCK), F32),
             pltpu.VMEM((count, BLOCK, BLOCK), BF16),
             pltpu.VMEM(tile, F32),
             pltpu.VMEM(tile, F32),
             pltpu.VMEM(tile, F32),
-            pltpu.VMEM(tile, F32),
-            pltpu.VMEM(tile, F32),
             pltpu.VMEM(state, F32),
             pltpu.VMEM(state, F32),
-            pltpu.VMEM(state, F32),
-            pltpu.VMEM(message, F32),
             pltpu.VMEM(message, F32),
             pltpu.VMEM((2, steps) + message, F32),
             pltpu.VMEM((2, steps) + message, F32),
             pltpu.VMEM((blocks, 8, LANES), F32),
             pltpu.VMEM((blocks, tp_count - 1, 8, LANES), F32),
             pltpu.VMEM((blocks, 2, BLOCK, LANES), F32),
+            pltpu.VMEM((tokens, width), BF16),
+            pltpu.VMEM((tokens, width), BF16),
+            pltpu.VMEM((tokens, width), BF16),
+            pltpu.VMEM((tokens, width), BF16),
+            pltpu.VMEM((tokens, width), BF16),
             pltpu.SemaphoreType.DMA((2, steps, heads)),
             pltpu.SemaphoreType.DMA((2, steps, heads)),
             pltpu.SemaphoreType.DMA((blocks, tp_count - 1)),
             pltpu.SemaphoreType.DMA((blocks, tp_count - 1)),
+            pltpu.SemaphoreType.DMA((5,)),
         ],
         compiler_params=pltpu.CompilerParams(
-            collective_id=0, has_side_effects=True, vmem_limit_bytes=56 * 1024 * 1024
+            collective_id=0, has_side_effects=True, vmem_limit_bytes=44 * 1024 * 1024
         ),
     )(
         offsets, query_rows, key_rows, value_rows, gate_logits,
         norm_gain.reshape(1, width), log_decay, cotangent,
     )
+    return pl.pallas_call(
+        functools.partial(finish_kernel, heads, blocks),
+        out_shape=(out,) * 5,
+        in_specs=[vmem] * 11,
+        out_specs=(anywhere,) * 5,
+        scratch_shapes=[
+            pltpu.VMEM((tokens, width), BF16),
+            pltpu.VMEM((tokens, width), BF16),
+            pltpu.VMEM((heads, D_HEAD, LANES), F32),
+            pltpu.SemaphoreType.DMA((3,)),
+            pltpu.SemaphoreType.DMA((blocks, 2)),
+        ],
+        compiler_params=pltpu.CompilerParams(vmem_limit_bytes=24 * 1024 * 1024),
+    )(key_rows, value_rows, *held)
 
 
 def solution(mesh):

time: 57.8 us -> 43.9 us (0.76)
  Pallas kernels: 48.7 us -> 40.9 us
  local copies, waits for them, and re-layouts: 8.13 us -> 2.05 us
    pallas_call x1, Pallas kernels: 48.7 us -> 37.4 us  [local(): pl.pallas_call(functools.partial(kernel, ctx_count, tp_count, heads, bloc...]
    unnamed x13 -> x10, local copies, waits for them, and re-layouts: 8.13 us -> 2.05 us
    pallas_call x0 -> x1, Pallas kernels: none -> 3.49 us  [local(): pl.pallas_call(functools.partial(finish_kernel, heads, blocks), out_shape...]
where the time goes in v2:
time: 43.9 us; the launch traced here: 43.6 us
  Pallas kernels  40.9 us (93%)
  local copies, waits for them, and re-layouts  2.05 us (5%)
  between operations  0.67 us (2%)
    pallas_call x1, Pallas kernels, local(): pl.pallas_call(functools.partial(kernel, ctx_count, tp_count, heads, bloc...  37.4 us
    pallas_call x1, Pallas kernels, local(): pl.pallas_call(functools.partial(finish_kernel, heads, blocks), out_shape...  3.49 us
    unnamed x10, local copies, waits for them, and re-layouts  2.05 us

profile of v2, /device:TPU:0, one launch (start us, length us, event | category | flops | bytes accessed | tf_op | source)
XLA Modules:
  0.0 43.6 jit_solution(2793696070605760203)
XLA Ops:
  0.6 0.0 copy-start.2
  0.6 0.7 %copy-done.2 = f32[4,1024]{1,0:T(4,128)S(1)} copy-done((f32[4,1024]{1,0:T(4,128)S(1)}, f32[4,1024]{1,0:T(4,128)}, u32[]{:S(2)}) %copy-start.2) | copy-done | bytes 16408
  1.4 0.0 copy-start.3
  1.4 0.7 %copy-done.3 = f32[512]{0:T(512)S(1)} copy-done((f32[512]{0:T(512)S(1)}, f32[512]{0:T(512)}, u32[]{:S(2)}) %copy-start.3) | copy-done | bytes 2072
  2.0 0.0 copy-start.4
  2.0 0.7 %copy-done.4 = s32[6]{0:T(128)S(1)} copy-done((s32[6]{0:T(128)S(1)}, s32[6]{0:T(128)}, u32[]{:S(2)}) %copy-start.4) | copy-done | bytes 48
  2.7 0.0 copy-start
  2.7 0.0 copy-start.1
  2.7 37.4 %shard_map.119 = (bf16[1024,512]{1,0:T(8,128)(2,1)S(1)}, bf16[1024,512]{1,0:T(8,128)(2,1)S(1)}, bf16[1024,512]{1,0:T(8,128)(2,1)S(1)}, f32[8,512,128]{2,1,0:T(8,...) custom-call(s32[6]{0:T(128)S(1)} %copy-done.4, ...), custom_call_target="tpu_custom_call" | custom-call | tf_op jit(solution)/shard_map/pallas_call | solution.py:414
  40.1 0.0 copy-done
  40.1 0.0 copy-done.1
  40.1 3.5 %shard_map.120 = (bf16[1024,512]{1,0:T(8,128)(2,1)}, bf16[1024,512]{1,0:T(8,128)(2,1)}, bf16[1024,512]{1,0:T(8,128)(2,1)}, bf16[1024,512]{1,0:T(8,128)(2,1)}, bf16[1024,512]{1,0:T(8,128)(2,1)}) custom-call(bf16[1024,512]{1,0:T(8,128)(2,1)S(1)} %copy-done, bf16[1024,512]{1,0:T(8,128)(2,1)S(1)} %copy-done.1, bf16[1024,512]{1,0:T(8,128)(2,1)S(1)} %get-tuple-element.14.att_in, ...), custom_call_target="tpu_custom_call" | custom-call | tf_op jit(solution)/shard_map/pallas_call | solution.py:465
Async XLA Ops:
  0.6 0.7 %copy-start.2 = (f32[4,1024]{1,0:T(4,128)S(1)}, f32[4,1024]{1,0:T(4,128)}, u32[]{:S(2)}) copy-start(f32[4,1024]{1,0:T(4,128)} %decay_ref.1) | copy-start | bytes 49156
  1.4 0.7 %copy-start.3 = (f32[512]{0:T(512)S(1)}, f32[512]{0:T(512)}, u32[]{:S(2)}) copy-start(f32[512]{0:T(512)} %param.12) | copy-start | bytes 6148
  2.0 0.7 %copy-start.4 = (s32[6]{0:T(128)S(1)}, s32[6]{0:T(128)}, u32[]{:S(2)}) copy-start(s32[6]{0:T(128)} %offs.1) | copy-start | bytes 76
  2.7 37.4 %copy-start = (bf16[1024,512]{1,0:T(8,128)(2,1)S(1)}, bf16[1024,512]{1,0:T(8,128)(2,1)}, u32[]{:S(2)}) copy-start(bf16[1024,512]{1,0:T(8,128)(2,1)} %k_ref.1) | copy-start | bytes 3145732
  2.7 37.4 %copy-start.1 = (bf16[1024,512]{1,0:T(8,128)(2,1)S(1)}, bf16[1024,512]{1,0:T(8,128)(2,1)}, u32[]{:S(2)}) copy-start(bf16[1024,512]{1,0:T(8,128)(2,1)} %v_ref.1) | copy-start | bytes 3145732

commit v3 on v2

--- a/solution.py
+++ b/solution.py
@@ -54,18 +54,19 @@
 
 def kernel(
     ctx_count, tp_count, heads, blocks,
-    offs, q_hbm, k_hbm, v_hbm, gate_hbm, gain_ref, decay_ref, cot_hbm,
+    offs_hbm, q_hbm, k_hbm, v_hbm, gate_hbm, gain_hbm, decay_hbm, cot_hbm,
     att_ref, dq_ref, dg_ref, key_acc, value_acc, last, factor, back_state, prefix,
     run_row, run_col, carry, bias, within, weights,
     attn, sig, gattn, states, local_state,
     total, send_state, recv_state, sums, recv_sums, scale_col,
-    q_ref, k_ref, v_ref, gate_ref, cot_ref,
+    offs, q_ref, k_ref, v_ref, gate_ref, gain_ref, decay_ref, cot_ref,
     send_sem, recv_sem, sum_send_sem, sum_recv_sem, load_sem,
 ):
     loads = [
         pltpu.make_async_copy(src, dst, load_sem.at[i])
         for i, (src, dst) in enumerate((
-            (k_hbm, k_ref), (v_hbm, v_ref), (q_hbm, q_ref), (gate_hbm, gate_ref), (cot_hbm, cot_ref),
+            (decay_hbm, decay_ref), (offs_hbm, offs), (k_hbm, k_ref), (v_hbm, v_ref),
+            (q_hbm, q_ref), (gate_hbm, gate_ref), (cot_hbm, cot_ref), (gain_hbm, gain_ref),
         ))
     ]
     for load in loads:
@@ -97,6 +98,8 @@
             count = count + (offs[entry] <= positions).astype(jnp.int32)
         return count
 
+    loads[0].wait()
+    loads[1].wait()
     decays = jnp.concatenate(
         [decay_ref[:, b * BLOCK:(b + 1) * BLOCK] for b in range(blocks)], axis=0
     )
@@ -190,14 +193,24 @@
             jnp.where(after, so_far_factor * other_factor, so_far_factor), (8, LANES)
         )
 
+    def join_early(way, h):
+        if steps > 1:
+            @pl.when(h > 0)
+            def _():
+                advance(way, 0, h - 1)
+
+            @pl.when(h == heads - 1)
+            def _():
+                advance(way, 0, h)
+
     def advance_rest(way):
         for step in range(1, steps - 1):
             for h in range(heads):
                 advance(way, step, h)
 
     pl.semaphore_wait(barrier, steps + tp_count - 1)
-    loads[0].wait()
-    loads[1].wait()
+    loads[2].wait()
+    loads[3].wait()
 
     def summarize(h, _):
         cols = head_cols(h)
@@ -214,12 +227,13 @@
         begin(0, h, acc, prod)
         return 0
 
-    lax.fori_loop(0, heads, summarize, 0)
-
-    loads[2].wait()
-    loads[3].wait()
+    lax.fori_loop(0, heads, summarize, 0, unroll=True)
+
+    loads[4].wait()
+    loads[5].wait()
     def attend(h, _):
         cols = head_cols(h)
+        join_early(0, h)
         for b in range(blocks):
             r = b * heads + h
             rows = block_rows(b)
@@ -235,13 +249,12 @@
                 weights[r, top:bottom, :bottom] = weight
                 attn[r, top:bottom, :] = mm(weight, value[:bottom])
             sig[r] = jax.nn.sigmoid(gate_ref[rows, cols].astype(F32))
-        if steps > 1:
-            advance(0, 0, h)
         return 0
 
-    lax.fori_loop(0, heads, attend, 0)
+    lax.fori_loop(0, heads, attend, 0, unroll=True)
     advance_rest(0)
-    loads[4].wait()
+    loads[6].wait()
+    loads[7].wait()
 
     def sum_copy(b, hop):
         return pltpu.make_async_remote_copy(
@@ -274,7 +287,7 @@
             return acc[0] + value * value, acc[1] + upstream(rows, cols, r) * value
 
         zero = jnp.zeros((BLOCK, LANES), F32)
-        squares, inners = lax.fori_loop(0, heads, carry_in, (zero, zero))
+        squares, inners = lax.fori_loop(0, heads, carry_in, (zero, zero), unroll=True)
         for at, part in ((0, squares), (chunks, inners)):
             line = mm_rt(ones, jnp.concatenate(split(part), axis=1))
             for c in range(chunks):
@@ -316,10 +329,11 @@
                 begin(1, h, acc, prod)
             return 0
 
-        lax.fori_loop(0, heads, grad_in, 0)
+        lax.fori_loop(0, heads, grad_in, 0, unroll=True)
 
     def retreat(h, _):
         cols = head_cols(h)
+        join_early(1, h)
         for b in range(blocks):
             r = b * heads + h
             rows = block_rows(b)
@@ -348,11 +362,9 @@
             key_acc[r, :HALF, :] += mm_lt(back[0], query[:HALF])
             value_acc[r] = mm_lt(weights[r, HALF:, :], high[HALF:])
             value_acc[r, :HALF, :] += mm_lt(weights[r, :HALF, :HALF], high[:HALF])
-        if steps > 1:
-            advance(1, 0, h)
         return 0
 
-    lax.fori_loop(0, heads, retreat, 0)
+    lax.fori_loop(0, heads, retreat, 0, unroll=True)
     advance_rest(1)
     if steps > 0:
         for h in range(heads):
@@ -389,7 +401,7 @@
             coming_ref[h] = factor[pl.ds(r, 1), :] * coming + back_state[r]
             return 0
 
-        lax.fori_loop(0, heads, finish, 0)
+        lax.fori_loop(0, heads, finish, 0, unroll=True)
         for i, (src, dst) in enumerate(((dk_ref, dk_out), (dv_ref, dv_out))):
             copy = pltpu.make_async_copy(src.at[rows, :], dst.at[rows, :], block_sem.at[b, i])
             copy.start()
@@ -424,7 +436,7 @@
             pltpu.VMEM(state, F32),
             pltpu.VMEM(message, F32),
         ),
-        in_specs=[pl.BlockSpec(memory_space=pltpu.SMEM)] + [anywhere] * 4 + [vmem] * 2 + [anywhere],
+        in_specs=[pl.BlockSpec(memory_space=pltpu.HBM)] * 8,
         out_specs=(vmem,) * 9,
         scratch_shapes=[
             pltpu.VMEM((count, BLOCK), F32),
@@ -444,24 +456,30 @@
             pltpu.VMEM((blocks, 8, LANES), F32),
             pltpu.VMEM((blocks, tp_count - 1, 8, LANES), F32),
             pltpu.VMEM((blocks, 2, BLOCK, LANES), F32),
-            pltpu.VMEM((tokens, width), BF16),
-            pltpu.VMEM((tokens, width), BF16),
-            pltpu.VMEM((tokens, width), BF16),
-            pltpu.VMEM((tokens, width), BF16),
+            pltpu.SMEM(offsets.shape, jnp.int32),
+            pltpu.VMEM((tokens, width), BF16),
+            pltpu.VMEM((tokens, width), BF16),
+            pltpu.VMEM((tokens, width), BF16),
+            pltpu.VMEM((tokens, width), BF16),
+            pltpu.VMEM((1, width), F32),
+            pltpu.VMEM(log_decay.shape, F32),
             pltpu.VMEM((tokens, width), BF16),
             pltpu.SemaphoreType.DMA((2, steps, heads)),
             pltpu.SemaphoreType.DMA((2, steps, heads)),
             pltpu.SemaphoreType.DMA((blocks, tp_count - 1)),
             pltpu.SemaphoreType.DMA((blocks, tp_count - 1)),
-            pltpu.SemaphoreType.DMA((5,)),
+            pltpu.SemaphoreType.DMA((8,)),
         ],
         compiler_params=pltpu.CompilerParams(
             collective_id=0, has_side_effects=True, vmem_limit_bytes=44 * 1024 * 1024
         ),
-    )(
-        offsets, query_rows, key_rows, value_rows, gate_logits,
-        norm_gain.reshape(1, width), log_decay, cotangent,
-    )
+    )(*[
+        pltpu.with_memory_space_constraint(array, pltpu.HBM)
+        for array in (
+            offsets, query_rows, key_rows, value_rows, gate_logits,
+            norm_gain.reshape(1, width), log_decay, cotangent,
+        )
+    ])
     return pl.pallas_call(
         functools.partial(finish_kernel, heads, blocks),
         out_shape=(out,) * 5,

time: 43.9 us -> 40.4 us (0.920)
  local copies, waits for them, and re-layouts: 2.05 us -> 0.01 us
  Pallas kernels: 40.9 us -> 39.4 us
    unnamed x10 -> x4, local copies, waits for them, and re-layouts: 2.05 us -> 0.01 us
    pallas_call x1, Pallas kernels: 37.4 us -> 36.2 us  [local(): pl.pallas_call(functools.partial(kernel, ctx_count, tp_count, heads, bloc...]
where the time goes in v3:
time: 40.4 us; the launch traced here: 40.2 us
  Pallas kernels  39.4 us (98%)
  between operations  0.83 us (2%)
    pallas_call x1, Pallas kernels, local(): pl.pallas_call(functools.partial(kernel, ctx_count, tp_count, heads, bloc...  36.2 us
    pallas_call x1, Pallas kernels, local(): pl.pallas_call(functools.partial(finish_kernel, heads, blocks), out_shape...  3.16 us

profile of v3, /device:TPU:0, one launch (start us, length us, event | category | flops | bytes accessed | tf_op | source)
XLA Modules:
  0.0 40.2 jit_solution(5602541360025611603)
XLA Ops:
  0.6 0.0 copy-start
  0.6 0.0 copy-start.1
  0.7 36.2 %shard_map.119 = (bf16[1024,512]{1,0:T(8,128)(2,1)S(1)}, bf16[1024,512]{1,0:T(8,128)(2,1)S(1)}, bf16[1024,512]{1,0:T(8,128)(2,1)S(1)}, f32[8,512,128]{2,1,0:T(8,...) custom-call(s32[6]{0:T(128)} %offs_hbm.1, ...), custom_call_target="tpu_custom_call" | custom-call | tf_op jit(solution)/shard_map/pallas_call | solution.py:426
  36.9 0.0 copy-done
  36.9 0.0 copy-done.1
  36.9 3.2 %shard_map.120 = (bf16[1024,512]{1,0:T(8,128)(2,1)}, bf16[1024,512]{1,0:T(8,128)(2,1)}, bf16[1024,512]{1,0:T(8,128)(2,1)}, bf16[1024,512]{1,0:T(8,128)(2,1)}, bf16[1024,512]{1,0:T(8,128)(2,1)}) custom-call(bf16[1024,512]{1,0:T(8,128)(2,1)S(1)} %copy-done, bf16[1024,512]{1,0:T(8,128)(2,1)S(1)} %copy-done.1, bf16[1024,512]{1,0:T(8,128)(2,1)S(1)} %get-tuple-element.14.att_in, ...), custom_call_target="tpu_custom_call" | custom-call | tf_op jit(solution)/shard_map/pallas_call | solution.py:483
Async XLA Ops:
  0.6 36.2 %copy-start = (bf16[1024,512]{1,0:T(8,128)(2,1)S(1)}, bf16[1024,512]{1,0:T(8,128)(2,1)}, u32[]{:S(2)}) copy-start(bf16[1024,512]{1,0:T(8,128)(2,1)} %k_ref.1) | copy-start | bytes 3145732
  0.6 36.2 %copy-start.1 = (bf16[1024,512]{1,0:T(8,128)(2,1)S(1)}, bf16[1024,512]{1,0:T(8,128)(2,1)}, u32[]{:S(2)}) copy-start(bf16[1024,512]{1,0:T(8,128)(2,1)} %v_ref.1) | copy-start | bytes 3145732

commit v4 on v3

--- a/solution.py
+++ b/solution.py
@@ -35,30 +35,33 @@
     return dot(left, right, ((1,), (1,)))
 
 
-def mm_lt(left, right):
-    return dot(left, right, ((0,), (0,)))
-
-
-def times_state(rows, state):
-    return mm(jnp.concatenate([rows, rows], axis=1), jnp.concatenate(split(state), axis=0))
-
-
-def times_state_t(rows, state):
-    return mm_rt(jnp.concatenate([rows, rows], axis=1), jnp.concatenate(split(state), axis=1))
-
-
-def outer_state(rows, weighted):
-    both = mm_lt(rows, jnp.concatenate(split(weighted), axis=1))
+def twice(rows):
+    return jnp.concatenate([rows, rows], axis=0)
+
+
+def state_times(state, columns):
+    return mm(jnp.concatenate(split(state), axis=1), twice(columns))
+
+
+def outer_state(columns, weighted):
+    both = mm_rt(columns, jnp.concatenate(split(weighted), axis=0))
     return both[:, :D_HEAD] + both[:, D_HEAD:]
+
+
+def causal(left, right, product):
+    first = product(left[:, :HALF], right[0])
+    second = product(left[:, HALF:], right[1])
+    return jnp.concatenate([first[:, :HALF], first[:, HALF:] + second], axis=1)
 
 
 def kernel(
     ctx_count, tp_count, heads, blocks,
     offs_hbm, q_hbm, k_hbm, v_hbm, gate_hbm, gain_hbm, decay_hbm, cot_hbm,
-    att_ref, dq_ref, dg_ref, key_acc, value_acc, last, factor, back_state, prefix,
+    att_ref, dq_ref, dg_ref, key_cols, value_cols, key_acc, value_acc, last, factor, back_state,
+    prefix,
     run_row, run_col, carry, bias, within, weights,
-    attn, sig, gattn, states, local_state,
-    total, send_state, recv_state, sums, recv_sums, scale_col,
+    query_cols, gain_cols, attn, sig, upstream, gattn, states, local_state,
+    total, send_state, recv_state, sums, recv_sums,
     offs, q_ref, k_ref, v_ref, gate_ref, gain_ref, decay_ref, cot_ref,
     send_sem, recv_sem, sum_send_sem, sum_recv_sem, load_sem,
 ):
@@ -124,21 +127,18 @@
         seg_col = segment(start + sub)
         before = segment(start - 1)
         final = segment(start + BLOCK - 1)
-        bias[b] = jnp.where((seg_col == seg_row) & (lower >= upper), 0.0, MASKED)
+        bias[b] = jnp.where((seg_col == seg_row) & (lower <= upper), 0.0, MASKED)
         carry_rows.append(jnp.where(seg_row == before, jnp.exp(rows), 0.0))
         end = rows[:, BLOCK - 1:]
         last_rows.append(jnp.where(seg_row == final, jnp.exp(jnp.minimum(end - rows, 0.0)), 0.0))
         whole = jnp.where(before == final, jnp.exp(end), 0.0)
         factor[b * heads:(b + 1) * heads, :] = jnp.broadcast_to(whole, (heads, LANES))
     count = heads * blocks
-    stacked = jnp.concatenate(
-        [running] + carry_rows + last_rows + [jnp.zeros((LANES - 3 * count, BLOCK), F32)], axis=0
-    )
-    columns = stacked.T
+    carry[...] = jnp.concatenate(carry_rows, axis=0)
+    last[...] = jnp.concatenate(last_rows, axis=0)
+    columns = jnp.concatenate([running, jnp.zeros((LANES - count, BLOCK), F32)], axis=0).T
     for r in range(count):
         run_col[r] = jnp.broadcast_to(columns[:, r:r + 1], (BLOCK, LANES))
-        carry[r] = jnp.broadcast_to(columns[:, count + r:count + r + 1], (BLOCK, LANES))
-        last[r] = jnp.broadcast_to(columns[:, 2 * count + r:2 * count + r + 1], (BLOCK, LANES))
 
     def head_cols(h):
         return pl.ds(pl.multiple_of(h * D_HEAD, D_HEAD), D_HEAD)
@@ -218,8 +218,11 @@
         prod = None
         for b in range(blocks):
             r = b * heads + h
-            weighted = v_ref[block_rows(b), cols].astype(F32) * last[r]
-            state = outer_state(k_ref[block_rows(b), cols], weighted)
+            key = k_ref[block_rows(b), cols].T
+            value = v_ref[block_rows(b), cols].T
+            key_cols[r] = key
+            value_cols[r] = value
+            state = outer_state(value, key.astype(F32) * last[pl.ds(r, 1), :])
             local_state[r] = state
             fac = factor_of(b, h)
             acc = state if acc is None else fac * acc + state
@@ -229,32 +232,39 @@
 
     lax.fori_loop(0, heads, summarize, 0, unroll=True)
 
-    loads[4].wait()
-    loads[5].wait()
+    for load in loads[4:]:
+        load.wait()
     def attend(h, _):
         cols = head_cols(h)
         join_early(0, h)
+        gain = jnp.broadcast_to(gain_ref[:, cols], (D_HEAD, LANES)).T
+        gain_cols[h] = gain
+        gain = jnp.concatenate([gain] * (BLOCK // LANES), axis=1)
         for b in range(blocks):
             r = b * heads + h
             rows = block_rows(b)
-            query, key, value = q_ref[rows, cols], k_ref[rows, cols], v_ref[rows, cols]
-            for top, bottom in ((0, HALF), (HALF, BLOCK)):
-                col = run_col[r, top:bottom, :]
-                col = jnp.concatenate([col] * (bottom // LANES), axis=1)
-                row = run_row[pl.ds(r, 1), :][:, :bottom]
-                decay = jnp.exp(jnp.minimum(col - row, bias[b, top:bottom, :bottom]))
-                within[r, top:bottom, :bottom] = decay
-                scores = mm_rt(query[top:bottom], key[:bottom])
+            query = q_ref[rows, cols].T
+            query_cols[r] = query
+            parts = []
+            for top in (0, HALF):
+                half = slice(top, top + HALF)
+                col = run_col[r, half, :]
+                col = jnp.concatenate([col] * ((BLOCK - top) // LANES), axis=1)
+                row = run_row[pl.ds(r, 1), :][:, top:]
+                decay = jnp.exp(jnp.minimum(row - col, bias[b, half, top:]))
+                within[r, half, top:] = decay
+                scores = mm(k_ref[pl.ds(b * BLOCK + top, HALF), cols], query[:, top:])
                 weight = (scores * decay).astype(BF16)
-                weights[r, top:bottom, :bottom] = weight
-                attn[r, top:bottom, :] = mm(weight, value[:bottom])
-            sig[r] = jax.nn.sigmoid(gate_ref[rows, cols].astype(F32))
+                weights[r, half, top:] = weight
+                parts.append(weight)
+            attn[r] = causal(value_cols[r], parts, mm)
+            gate = jax.nn.sigmoid(gate_ref[rows, cols].T.astype(F32))
+            sig[r] = gate
+            upstream[r] = cot_ref[rows, cols].T.astype(F32) * (gain * gate)
         return 0
 
     lax.fori_loop(0, heads, attend, 0, unroll=True)
     advance_rest(0)
-    loads[6].wait()
-    loads[7].wait()
 
     def sum_copy(b, hop):
         return pltpu.make_async_remote_copy(
@@ -266,60 +276,49 @@
             device_id_type=MESH,
         )
 
-    def upstream(rows, cols, r):
-        return cot_ref[rows, cols].astype(F32) * (gain_ref[:, cols] * sig[r])
-
-    ones = jnp.ones((8, 2 * LANES), BF16)
     chunks = BLOCK // LANES
     for b in range(blocks):
-        rows = block_rows(b)
-
-        def carry_in(h, acc, b=b, rows=rows):
-            cols = head_cols(h)
+        def carry_in(h, acc, b=b):
             r = b * heads + h
             if b == 0 and steps > 0:
                 advance(0, steps - 1, h)
             state = prefix[h, :D_HEAD, :]
             states[r] = state
-            value = attn[r] + carry[r] * times_state(q_ref[rows, cols], state)
+            value = attn[r] + carry[pl.ds(r, 1), :] * state_times(state, query_cols[r])
             attn[r] = value
             prefix[h, :D_HEAD, :] = factor_of(b, h) * state + local_state[r]
-            return acc[0] + value * value, acc[1] + upstream(rows, cols, r) * value
-
-        zero = jnp.zeros((BLOCK, LANES), F32)
+            return (
+                acc[0] + jnp.sum(value * value, axis=0, keepdims=True),
+                acc[1] + jnp.sum(upstream[r] * value, axis=0, keepdims=True),
+            )
+
+        zero = jnp.zeros((1, BLOCK), F32)
         squares, inners = lax.fori_loop(0, heads, carry_in, (zero, zero), unroll=True)
-        for at, part in ((0, squares), (chunks, inners)):
-            line = mm_rt(ones, jnp.concatenate(split(part), axis=1))
+        for at, line in ((0, squares), (chunks, inners)):
             for c in range(chunks):
                 sums[b, at + c:at + c + 1, :] = line[:1, c * LANES:(c + 1) * LANES]
         for hop in range(1, tp_count):
             sum_copy(b, hop).start()
 
+    scales = []
     for b in range(blocks):
-        rows = block_rows(b)
         added = sums[b]
         for hop in range(1, tp_count):
             sum_copy(b, hop).wait()
             added = added + recv_sums[b, hop - 1]
         inverse = 1.0 / jnp.sqrt(added[:chunks] / features + EPS_NORM)
         mean_inner = added[chunks:] * inverse / features
-        turned = jnp.concatenate(
-            [inverse, mean_inner, jnp.zeros((LANES - 2 * chunks, LANES), F32)], axis=0
-        ).T
-        for c in range(chunks):
-            here = pl.ds(c * LANES, LANES)
-            scale_col[b, 0, here, :] = jnp.broadcast_to(turned[:, c:c + 1], (LANES, LANES))
-            scale_col[b, 1, here, :] = jnp.broadcast_to(
-                turned[:, chunks + c:chunks + c + 1], (LANES, LANES)
-            )
-
-        def grad_in(h, _, b=b, rows=rows):
-            cols = head_cols(h)
+        inv, mean_inner = (
+            jnp.concatenate([part[c:c + 1] for c in range(chunks)], axis=1)
+            for part in (inverse, mean_inner)
+        )
+        scales.append(inv)
+
+        def grad_in(h, _, b=b, inv=inv, mean_inner=mean_inner):
             r = b * heads + h
-            inv = scale_col[b, 0]
-            grad = (upstream(rows, cols, r) - attn[r] * inv * scale_col[b, 1]) * inv
+            grad = (upstream[r] - attn[r] * (inv * mean_inner)) * inv
             gattn[r] = grad
-            back_state[r] = outer_state(q_ref[rows, cols], grad * carry[r])
+            back_state[r] = outer_state(query_cols[r], grad * carry[pl.ds(r, 1), :])
             if b == blocks - 1:
                 acc = back_state[r]
                 prod = factor_of(b, h)
@@ -334,34 +333,32 @@
     def retreat(h, _):
         cols = head_cols(h)
         join_early(1, h)
+        gain = jnp.concatenate([gain_cols[h]] * (BLOCK // LANES), axis=1)
         for b in range(blocks):
             r = b * heads + h
             rows = block_rows(b)
-            query, key, value = q_ref[rows, cols], k_ref[rows, cols], v_ref[rows, cols]
-            normed = attn[r] * scale_col[b, 0]
+            high, low = split(gattn[r])
+            parts = []
+            for top in (0, HALF):
+                half = slice(top, top + HALF)
+                scores = mm(v_ref[pl.ds(b * BLOCK + top, HALF), cols], high[:, top:])
+                parts.append((scores * within[r, half, top:]).astype(BF16))
+            state_high, state_low = split(states[r].T)
+            crossed = mm(
+                jnp.concatenate([state_high, state_high], axis=1),
+                jnp.concatenate([high, low], axis=0),
+            ) + mm(state_low, high)
+            dq = causal(key_cols[r], parts, mm) + carry[pl.ds(r, 1), :] * crossed
+            dq_ref[rows, cols] = dq.astype(BF16).T
+            query = query_cols[r]
+            key_acc[r, :, :HALF] = mm_rt(query, parts[0])
+            key_acc[r, :, HALF:] = mm_rt(query[:, HALF:], parts[1])
+            value_acc[r, :, :HALF] = mm_rt(high, weights[r, :HALF, :])
+            value_acc[r, :, HALF:] = mm_rt(high[:, HALF:], weights[r, HALF:, HALF:])
+            normed = attn[r] * scales[b]
             gate = sig[r]
-            gated = normed * (gain_ref[:, cols] * gate)
-            att_ref[rows, cols] = gated.astype(BF16)
-            dg_ref[rows, cols] = (cot_ref[rows, cols].astype(F32) * gated * (1.0 - gate)).astype(BF16)
-            high, low = split(gattn[r])
-            state_high, state_low = split(states[r])
-            crossed = mm_rt(
-                jnp.concatenate([high, low], axis=1),
-                jnp.concatenate([state_high, state_high], axis=1),
-            ) + mm_rt(high, state_low)
-            crossed = carry[r] * crossed
-            back = []
-            for top, bottom in ((0, HALF), (HALF, BLOCK)):
-                scores = mm_rt(high[top:bottom], value[:bottom])
-                piece = (scores * within[r, top:bottom, :bottom]).astype(BF16)
-                back.append(piece)
-                dq_ref[pl.ds(b * BLOCK + top, HALF), cols] = (
-                    mm(piece, key[:bottom]) + crossed[top:bottom]
-                ).astype(BF16)
-            key_acc[r] = mm_lt(back[1], query[HALF:])
-            key_acc[r, :HALF, :] += mm_lt(back[0], query[:HALF])
-            value_acc[r] = mm_lt(weights[r, HALF:, :], high[HALF:])
-            value_acc[r, :HALF, :] += mm_lt(weights[r, :HALF, :HALF], high[:HALF])
+            att_ref[rows, cols] = (normed * (gain * gate)).astype(BF16).T
+            dg_ref[rows, cols] = (upstream[r] * normed * (1.0 - gate)).astype(BF16).T
         return 0
 
     lax.fori_loop(0, heads, retreat, 0, unroll=True)
@@ -373,7 +370,8 @@
 
 def finish_kernel(
     heads, blocks,
-    k_ref, v_ref, att_in, dq_in, dg_in, key_acc, value_acc, last, factor, back_state, prefix,
+    att_in, dq_in, dg_in, key_cols, value_cols, key_acc, value_acc, last, factor, back_state,
+    prefix,
     att_out, dq_out, dk_out, dv_out, dg_out,
     dk_ref, dv_ref, coming_ref, ready_sem, block_sem,
 ):
@@ -392,12 +390,11 @@
             cols = pl.ds(pl.multiple_of(h * D_HEAD, D_HEAD), D_HEAD)
             r = b * heads + h
             coming = coming_ref[h]
-            dk_ref[rows, cols] = (
-                key_acc[r] + last[r] * times_state_t(v_ref[rows, cols], coming)
-            ).astype(BF16)
-            dv_ref[rows, cols] = (
-                value_acc[r] + last[r] * times_state(k_ref[rows, cols], coming)
-            ).astype(BF16)
+            weight = last[pl.ds(r, 1), :]
+            dk = key_acc[r] + weight * state_times(coming, value_cols[r])
+            dv = value_acc[r] + weight * state_times(coming.T, key_cols[r])
+            dk_ref[rows, cols] = dk.astype(BF16).T
+            dv_ref[rows, cols] = dv.astype(BF16).T
             coming_ref[h] = factor[pl.ds(r, 1), :] * coming + back_state[r]
             return 0
 
@@ -420,7 +417,7 @@
     out = jax.ShapeDtypeStruct((tokens, width), BF16)
     vmem = pl.BlockSpec(memory_space=pltpu.VMEM)
     anywhere = pl.BlockSpec(memory_space=pl.ANY)
-    tile = (count, BLOCK, LANES)
+    tile = (count, D_HEAD, BLOCK)
     state = (count, D_HEAD, D_HEAD)
     message = (heads, D_HEAD + 8, LANES)
     held = pl.pallas_call(
@@ -429,22 +426,27 @@
             pltpu.VMEM((tokens, width), BF16),
             pltpu.VMEM((tokens, width), BF16),
             pltpu.VMEM((tokens, width), BF16),
+            pltpu.VMEM(tile, BF16),
+            pltpu.VMEM(tile, BF16),
             pltpu.VMEM(tile, F32),
             pltpu.VMEM(tile, F32),
-            pltpu.VMEM(tile, F32),
+            pltpu.VMEM((count, BLOCK), F32),
             pltpu.VMEM((count, LANES), F32),
             pltpu.VMEM(state, F32),
             pltpu.VMEM(message, F32),
         ),
         in_specs=[pl.BlockSpec(memory_space=pltpu.HBM)] * 8,
-        out_specs=(vmem,) * 9,
+        out_specs=(vmem,) * 11,
         scratch_shapes=[
             pltpu.VMEM((count, BLOCK), F32),
-            pltpu.VMEM(tile, F32),
-            pltpu.VMEM(tile, F32),
+            pltpu.VMEM((count, BLOCK, LANES), F32),
+            pltpu.VMEM((count, BLOCK), F32),
             pltpu.VMEM((blocks, BLOCK, BLOCK), F32),
             pltpu.VMEM((count, BLOCK, BLOCK), F32),
             pltpu.VMEM((count, BLOCK, BLOCK), BF16),
+            pltpu.VMEM(tile, BF16),
+            pltpu.VMEM((heads, D_HEAD, LANES), F32),
+            pltpu.VMEM(tile, F32),
             pltpu.VMEM(tile, F32),
             pltpu.VMEM(tile, F32),
             pltpu.VMEM(tile, F32),
@@ -455,7 +457,6 @@
             pltpu.VMEM((2, steps) + message, F32),
             pltpu.VMEM((blocks, 8, LANES), F32),
             pltpu.VMEM((blocks, tp_count - 1, 8, LANES), F32),
-            pltpu.VMEM((blocks, 2, BLOCK, LANES), F32),
             pltpu.SMEM(offsets.shape, jnp.int32),
             pltpu.VMEM((tokens, width), BF16),
             pltpu.VMEM((tokens, width), BF16),
@@ -493,7 +494,7 @@
             pltpu.SemaphoreType.DMA((blocks, 2)),
         ],
         compiler_params=pltpu.CompilerParams(vmem_limit_bytes=24 * 1024 * 1024),
-    )(key_rows, value_rows, *held)
+    )(*held)
 
 
 def solution(mesh):

time: 40.4 us -> 37.7 us (0.933)
  Pallas kernels: 39.4 us -> 36.9 us
    pallas_call x1, Pallas kernels: 36.2 us -> 33.8 us  [local(): pl.pallas_call(functools.partial(kernel, ctx_count, tp_count, heads, bloc...]
where the time goes in v4:
time: 37.7 us; the launch traced here: 37.5 us
  Pallas kernels  36.9 us (98%)
  between operations  0.64 us (2%)
    pallas_call x1, Pallas kernels, local(): pl.pallas_call(functools.partial(kernel, ctx_count, tp_count, heads, bloc...  33.8 us
    pallas_call x1, Pallas kernels, local(): pl.pallas_call(functools.partial(finish_kernel, heads, blocks), out_shape...  3.05 us

profile of v4, /device:TPU:0, one launch (start us, length us, event | category | flops | bytes accessed | tf_op | source)
XLA Modules:
  0.0 37.5 jit_solution(8349929127773193373)
XLA Ops:
  0.6 33.8 %shard_map.119 = (bf16[1024,512]{1,0:T(8,128)(2,1)S(1)}, bf16[1024,512]{1,0:T(8,128)(2,1)S(1)}, bf16[1024,512]{1,0:T(8,128)(2,1)S(1)}, bf16[8,128,512]{2,1,0:T(8...) custom-call(s32[6]{0:T(128)} %offs_hbm.1, ...), custom_call_target="tpu_custom_call" | custom-call | tf_op jit(solution)/shard_map/pallas_call | solution.py:423
  34.4 3.1 %shard_map.120 = (bf16[1024,512]{1,0:T(8,128)(2,1)}, bf16[1024,512]{1,0:T(8,128)(2,1)}, bf16[1024,512]{1,0:T(8,128)(2,1)}, bf16[1024,512]{1,0:T(8,128)(2,1)}, bf16[1024,512]{1,0:T(8,128)(2,1)}) custom-call(bf16[1024,512]{1,0:T(8,128)(2,1)S(1)} %get-tuple-element.16.att_in, bf16[1024,512]{1,0:T(8,128)(2,1)S(1)} %get-tuple-element.17.dq_in, ...), custom_call_target="tpu_custom_call" | custom-call | tf_op jit(solution)/shard_map/pallas_call | solution.py:484

commit v5 on v4

--- a/solution.py
+++ b/solution.py
@@ -57,8 +57,8 @@
 def kernel(
     ctx_count, tp_count, heads, blocks,
     offs_hbm, q_hbm, k_hbm, v_hbm, gate_hbm, gain_hbm, decay_hbm, cot_hbm,
-    att_ref, dq_ref, dg_ref, key_cols, value_cols, key_acc, value_acc, last, factor, back_state,
-    prefix,
+    att_ref, dq_ref, dk_ref, dv_ref, dg_ref,
+    key_cols, value_cols, key_acc, value_acc, last, factor, back_state, prefix,
     run_row, run_col, carry, bias, within, weights,
     query_cols, gain_cols, attn, sig, upstream, gattn, states, local_state,
     total, send_state, recv_state, sums, recv_sums,
@@ -119,27 +119,19 @@
     run_row[...] = running
     lane = lax.broadcasted_iota(jnp.int32, (1, BLOCK), 1)
     sub = lax.broadcasted_iota(jnp.int32, (BLOCK, 1), 0)
-    carry_rows, last_rows = [], []
+    last_rows = []
     for b in range(blocks):
         start = first + b * BLOCK
         rows = running[b * heads:(b + 1) * heads]
         seg_row = segment(start + lane)
-        seg_col = segment(start + sub)
         before = segment(start - 1)
         final = segment(start + BLOCK - 1)
-        bias[b] = jnp.where((seg_col == seg_row) & (lower <= upper), 0.0, MASKED)
-        carry_rows.append(jnp.where(seg_row == before, jnp.exp(rows), 0.0))
         end = rows[:, BLOCK - 1:]
         last_rows.append(jnp.where(seg_row == final, jnp.exp(jnp.minimum(end - rows, 0.0)), 0.0))
         whole = jnp.where(before == final, jnp.exp(end), 0.0)
         factor[b * heads:(b + 1) * heads, :] = jnp.broadcast_to(whole, (heads, LANES))
     count = heads * blocks
-    carry[...] = jnp.concatenate(carry_rows, axis=0)
     last[...] = jnp.concatenate(last_rows, axis=0)
-    columns = jnp.concatenate([running, jnp.zeros((LANES - count, BLOCK), F32)], axis=0).T
-    for r in range(count):
-        run_col[r] = jnp.broadcast_to(columns[:, r:r + 1], (BLOCK, LANES))
-
     def head_cols(h):
         return pl.ds(pl.multiple_of(h * D_HEAD, D_HEAD), D_HEAD)
 
@@ -232,6 +224,19 @@
 
     lax.fori_loop(0, heads, summarize, 0, unroll=True)
 
+    carry_rows = []
+    for b in range(blocks):
+        start = first + b * BLOCK
+        seg_row = segment(start + lane)
+        seg_col = segment(start + sub)
+        bias[b] = jnp.where((seg_col == seg_row) & (lower <= upper), 0.0, MASKED)
+        rows = running[b * heads:(b + 1) * heads]
+        carry_rows.append(jnp.where(seg_row == segment(start - 1), jnp.exp(rows), 0.0))
+    carry[...] = jnp.concatenate(carry_rows, axis=0)
+    columns = jnp.concatenate([running, jnp.zeros((LANES - count, BLOCK), F32)], axis=0).T
+    for r in range(count):
+        run_col[r] = jnp.broadcast_to(columns[:, r:r + 1], (BLOCK, LANES))
+
     for load in loads[4:]:
         load.wait()
     def attend(h, _):
@@ -266,69 +271,72 @@
     lax.fori_loop(0, heads, attend, 0, unroll=True)
     advance_rest(0)
 
-    def sum_copy(b, hop):
+    def sum_copy(hop):
         return pltpu.make_async_remote_copy(
-            src_ref=sums.at[b],
-            dst_ref=recv_sums.at[b, hop - 1],
-            send_sem=sum_send_sem.at[b, hop - 1],
-            recv_sem=sum_recv_sem.at[b, hop - 1],
+            src_ref=sums,
+            dst_ref=recv_sums.at[hop - 1],
+            send_sem=sum_send_sem.at[hop - 1],
+            recv_sem=sum_recv_sem.at[hop - 1],
             device_id=(ctx, peer(hop)),
             device_id_type=MESH,
         )
 
     chunks = BLOCK // LANES
-    for b in range(blocks):
-        def carry_in(h, acc, b=b):
-            r = b * heads + h
-            if b == 0 and steps > 0:
-                advance(0, steps - 1, h)
-            state = prefix[h, :D_HEAD, :]
+
+    def carry_in(h, acc):
+        if steps > 0:
+            advance(0, steps - 1, h)
+        state = prefix[h, :D_HEAD, :]
+        added = []
+        for b in range(blocks):
+            r = b * heads + h
             states[r] = state
             value = attn[r] + carry[pl.ds(r, 1), :] * state_times(state, query_cols[r])
             attn[r] = value
-            prefix[h, :D_HEAD, :] = factor_of(b, h) * state + local_state[r]
-            return (
-                acc[0] + jnp.sum(value * value, axis=0, keepdims=True),
-                acc[1] + jnp.sum(upstream[r] * value, axis=0, keepdims=True),
-            )
-
-        zero = jnp.zeros((1, BLOCK), F32)
-        squares, inners = lax.fori_loop(0, heads, carry_in, (zero, zero), unroll=True)
-        for at, line in ((0, squares), (chunks, inners)):
-            for c in range(chunks):
-                sums[b, at + c:at + c + 1, :] = line[:1, c * LANES:(c + 1) * LANES]
-        for hop in range(1, tp_count):
-            sum_copy(b, hop).start()
-
-    scales = []
+            if b + 1 < blocks:
+                state = factor_of(b, h) * state + local_state[r]
+            added.append(acc[2 * b] + jnp.sum(value * value, axis=0, keepdims=True))
+            added.append(acc[2 * b + 1] + jnp.sum(upstream[r] * value, axis=0, keepdims=True))
+        return tuple(added)
+
+    zero = jnp.zeros((1, BLOCK), F32)
+    lines = lax.fori_loop(0, heads, carry_in, (zero,) * (2 * blocks), unroll=True)
+    for at, line in enumerate(lines):
+        for c in range(chunks):
+            sums[at, c:c + 1, :] = line[:, c * LANES:(c + 1) * LANES]
+    for hop in range(1, tp_count):
+        sum_copy(hop).start()
+    added = sums[...]
+    for hop in range(1, tp_count):
+        sum_copy(hop).wait()
+        added = added + recv_sums[hop - 1]
+    scales, inner_scales = [], []
     for b in range(blocks):
-        added = sums[b]
-        for hop in range(1, tp_count):
-            sum_copy(b, hop).wait()
-            added = added + recv_sums[b, hop - 1]
-        inverse = 1.0 / jnp.sqrt(added[:chunks] / features + EPS_NORM)
-        mean_inner = added[chunks:] * inverse / features
+        inverse = 1.0 / jnp.sqrt(added[2 * b] / features + EPS_NORM)
+        mean_inner = added[2 * b + 1] * inverse / features
         inv, mean_inner = (
             jnp.concatenate([part[c:c + 1] for c in range(chunks)], axis=1)
             for part in (inverse, mean_inner)
         )
         scales.append(inv)
-
-        def grad_in(h, _, b=b, inv=inv, mean_inner=mean_inner):
-            r = b * heads + h
-            grad = (upstream[r] - attn[r] * (inv * mean_inner)) * inv
+        inner_scales.append(inv * mean_inner)
+
+    def grad_in(h, _):
+        acc = None
+        prod = None
+        for b in range(blocks - 1, -1, -1):
+            r = b * heads + h
+            grad = (upstream[r] - attn[r] * inner_scales[b]) * scales[b]
             gattn[r] = grad
-            back_state[r] = outer_state(query_cols[r], grad * carry[pl.ds(r, 1), :])
-            if b == blocks - 1:
-                acc = back_state[r]
-                prod = factor_of(b, h)
-                for e in range(blocks - 2, -1, -1):
-                    acc = factor_of(e, h) * acc + back_state[e * heads + h]
-                    prod = prod * factor_of(e, h)
-                begin(1, h, acc, prod)
-            return 0
-
-        lax.fori_loop(0, heads, grad_in, 0, unroll=True)
+            state = outer_state(query_cols[r], grad * carry[pl.ds(r, 1), :])
+            back_state[r] = state
+            fac = factor_of(b, h)
+            acc = state if acc is None else fac * acc + state
+            prod = fac if prod is None else prod * fac
+        begin(1, h, acc, prod)
+        return 0
+
+    lax.fori_loop(0, heads, grad_in, 0, unroll=True)
 
     def retreat(h, _):
         cols = head_cols(h)
@@ -363,47 +371,34 @@
 
     lax.fori_loop(0, heads, retreat, 0, unroll=True)
     advance_rest(1)
-    if steps > 0:
-        for h in range(heads):
+
+    def finish(h, _):
+        cols = head_cols(h)
+        if steps > 0:
             advance(1, steps - 1, h)
-
-
-def finish_kernel(
-    heads, blocks,
-    att_in, dq_in, dg_in, key_cols, value_cols, key_acc, value_acc, last, factor, back_state,
-    prefix,
-    att_out, dq_out, dk_out, dv_out, dg_out,
-    dk_ref, dv_ref, coming_ref, ready_sem, block_sem,
-):
-    ready = [
-        pltpu.make_async_copy(src, dst, ready_sem.at[i])
-        for i, (src, dst) in enumerate(((att_in, att_out), (dq_in, dq_out), (dg_in, dg_out)))
-    ]
-    for copy in ready:
-        copy.start()
-    for h in range(heads):
-        coming_ref[h] = prefix[h, :D_HEAD, :]
-    for b in range(blocks - 1, -1, -1):
-        rows = pl.ds(b * BLOCK, BLOCK)
-
-        def finish(h, _, b=b, rows=rows):
-            cols = pl.ds(pl.multiple_of(h * D_HEAD, D_HEAD), D_HEAD)
-            r = b * heads + h
-            coming = coming_ref[h]
+        coming = prefix[h, :D_HEAD, :]
+        for b in range(blocks - 1, -1, -1):
+            r = b * heads + h
+            rows = block_rows(b)
             weight = last[pl.ds(r, 1), :]
             dk = key_acc[r] + weight * state_times(coming, value_cols[r])
             dv = value_acc[r] + weight * state_times(coming.T, key_cols[r])
             dk_ref[rows, cols] = dk.astype(BF16).T
             dv_ref[rows, cols] = dv.astype(BF16).T
-            coming_ref[h] = factor[pl.ds(r, 1), :] * coming + back_state[r]
-            return 0
-
-        lax.fori_loop(0, heads, finish, 0, unroll=True)
-        for i, (src, dst) in enumerate(((dk_ref, dk_out), (dv_ref, dv_out))):
-            copy = pltpu.make_async_copy(src.at[rows, :], dst.at[rows, :], block_sem.at[b, i])
-            copy.start()
-            ready.append(copy)
-    for copy in ready:
+            if b > 0:
+                coming = factor_of(b, h) * coming + back_state[r]
+        return 0
+
+    lax.fori_loop(0, heads, finish, 0, unroll=True)
+
+
+def write_kernel(count, *refs):
+    copies = [
+        pltpu.make_async_copy(refs[i], refs[count + i], refs[2 * count].at[i]) for i in range(count)
+    ]
+    for copy in copies:
+        copy.start()
+    for copy in copies:
         copy.wait()
 
 
@@ -422,10 +417,10 @@
     message = (heads, D_HEAD + 8, LANES)
     held = pl.pallas_call(
         functools.partial(kernel, ctx_count, tp_count, heads, blocks),
-        out_shape=(
-            pltpu.VMEM((tokens, width), BF16),
-            pltpu.VMEM((tokens, width), BF16),
-            pltpu.VMEM((tokens, width), BF16),
+        out_shape=(pltpu.VMEM((tokens, width), BF16),) * 5,
+        in_specs=[pl.BlockSpec(memory_space=pltpu.HBM)] * 8,
+        out_specs=(vmem,) * 5,
+        scratch_shapes=[
             pltpu.VMEM(tile, BF16),
             pltpu.VMEM(tile, BF16),
             pltpu.VMEM(tile, F32),
@@ -434,10 +429,6 @@
             pltpu.VMEM((count, LANES), F32),
             pltpu.VMEM(state, F32),
             pltpu.VMEM(message, F32),
-        ),
-        in_specs=[pl.BlockSpec(memory_space=pltpu.HBM)] * 8,
-        out_specs=(vmem,) * 11,
-        scratch_shapes=[
             pltpu.VMEM((count, BLOCK), F32),
             pltpu.VMEM((count, BLOCK, LANES), F32),
             pltpu.VMEM((count, BLOCK), F32),
@@ -455,8 +446,8 @@
             pltpu.VMEM(message, F32),
             pltpu.VMEM((2, steps) + message, F32),
             pltpu.VMEM((2, steps) + message, F32),
-            pltpu.VMEM((blocks, 8, LANES), F32),
-            pltpu.VMEM((blocks, tp_count - 1, 8, LANES), F32),
+            pltpu.VMEM((2 * blocks, BLOCK // LANES, LANES), F32),
+            pltpu.VMEM((tp_count - 1, 2 * blocks, BLOCK // LANES, LANES), F32),
             pltpu.SMEM(offsets.shape, jnp.int32),
             pltpu.VMEM((tokens, width), BF16),
             pltpu.VMEM((tokens, width), BF16),
@@ -467,12 +458,12 @@
             pltpu.VMEM((tokens, width), BF16),
             pltpu.SemaphoreType.DMA((2, steps, heads)),
             pltpu.SemaphoreType.DMA((2, steps, heads)),
-            pltpu.SemaphoreType.DMA((blocks, tp_count - 1)),
-            pltpu.SemaphoreType.DMA((blocks, tp_count - 1)),
+            pltpu.SemaphoreType.DMA((tp_count - 1,)),
+            pltpu.SemaphoreType.DMA((tp_count - 1,)),
             pltpu.SemaphoreType.DMA((8,)),
         ],
         compiler_params=pltpu.CompilerParams(
-            collective_id=0, has_side_effects=True, vmem_limit_bytes=44 * 1024 * 1024
+            collective_id=0, has_side_effects=True, vmem_limit_bytes=52 * 1024 * 1024
         ),
     )(*[
         pltpu.with_memory_space_constraint(array, pltpu.HBM)
@@ -482,18 +473,11 @@
         )
     ])
     return pl.pallas_call(
-        functools.partial(finish_kernel, heads, blocks),
+        functools.partial(write_kernel, 5),
         out_shape=(out,) * 5,
-        in_specs=[vmem] * 11,
+        in_specs=[vmem] * 5,
         out_specs=(anywhere,) * 5,
-        scratch_shapes=[
-            pltpu.VMEM((tokens, width), BF16),
-            pltpu.VMEM((tokens, width), BF16),
-            pltpu.VMEM((heads, D_HEAD, LANES), F32),
-            pltpu.SemaphoreType.DMA((3,)),
-            pltpu.SemaphoreType.DMA((blocks, 2)),
-        ],
-        compiler_params=pltpu.CompilerParams(vmem_limit_bytes=24 * 1024 * 1024),
+        scratch_shapes=[pltpu.SemaphoreType.DMA((5,))],
     )(*held)
 
 

time: 37.7 us -> 43.6 us (1.16)
  local copies, waits for them, and re-layouts: 0 us -> 4.93 us
  Pallas kernels: 36.9 us -> 37.8 us
    unnamed x0 -> x10, local copies, waits for them, and re-layouts: none -> 4.93 us
    pallas_call x1, Pallas kernels: 3.05 us -> 4.88 us  [local(): pl.pallas_call(functools.partial(write_kernel, 5), out_shape=(out,) * 5,...]
    pallas_call x1, Pallas kernels: 33.8 us -> 32.9 us  [local(): pl.pallas_call(functools.partial(kernel, ctx_count, tp_count, heads, bloc...]
where the time goes in v5:
time: 43.6 us; the launch traced here: 43.4 us
  Pallas kernels  37.8 us (87%)
  local copies, waits for them, and re-layouts  4.93 us (11%)
  between operations  0.65 us (1%)
    pallas_call x1, Pallas kernels, local(): pl.pallas_call(functools.partial(kernel, ctx_count, tp_count, heads, bloc...  32.9 us
    unnamed x10, local copies, waits for them, and re-layouts  4.93 us
    pallas_call x1, Pallas kernels, local(): pl.pallas_call(functools.partial(write_kernel, 5), out_shape=(out,) * 5,...  4.88 us

profile of v5, /device:TPU:0, one launch (start us, length us, event | category | flops | bytes accessed | tf_op | source)
XLA Modules:
  0.0 43.4 jit_solution(16405909531926125258)
XLA Ops:
  0.6 32.9 %shard_map.119 = (bf16[1024,512]{1,0:T(8,128)(2,1)S(1)}, bf16[1024,512]{1,0:T(8,128)(2,1)S(1)}, bf16[1024,512]{1,0:T(8,128)(2,1)S(1)}, bf16[1024,512]{1,0:T(8,128)(2,1)S(1)}, bf16[1024,512]{1,0:T(8,128)(2,1)S(1)}) custom-call(s32[6]{0:T(128)} %offs_hbm.1, bf16[1024,512]{1,0:T(8,128)(2,1)} %q_hbm.1, bf16[1024,512]{1,0:T(8,128)(2,1)} %k_hbm.1, ...), custom_call_target="tpu_custom_call" | custom-call | tf_op jit(solution)/shard_map/pallas_call | solution.py:418
  33.6 0.0 copy-start
  33.6 1.0 %copy-done = bf16[1024,512]{1,0:T(8,128)(2,1)} copy-done((bf16[1024,512]{1,0:T(8,128)(2,1)}, bf16[1024,512]{1,0:T(8,128)(2,1)S(1)}, u32[]{:S(2)}) %copy-start) | copy-done | bytes 1048600
  34.5 0.0 copy-start.1
  34.5 1.0 %copy-done.1 = bf16[1024,512]{1,0:T(8,128)(2,1)} copy-done((bf16[1024,512]{1,0:T(8,128)(2,1)}, bf16[1024,512]{1,0:T(8,128)(2,1)S(1)}, u32[]{:S(2)}) %copy-start.1) | copy-done | bytes 1048600
  35.6 0.0 copy-start.2
  35.6 1.0 %copy-done.2 = bf16[1024,512]{1,0:T(8,128)(2,1)} copy-done((bf16[1024,512]{1,0:T(8,128)(2,1)}, bf16[1024,512]{1,0:T(8,128)(2,1)S(1)}, u32[]{:S(2)}) %copy-start.2) | copy-done | bytes 1048600
  36.6 0.0 copy-start.3
  36.6 1.0 %copy-done.3 = bf16[1024,512]{1,0:T(8,128)(2,1)} copy-done((bf16[1024,512]{1,0:T(8,128)(2,1)}, bf16[1024,512]{1,0:T(8,128)(2,1)S(1)}, u32[]{:S(2)}) %copy-start.3) | copy-done | bytes 1048600
  37.5 0.0 copy-start.4
  37.5 1.0 %copy-done.4 = bf16[1024,512]{1,0:T(8,128)(2,1)} copy-done((bf16[1024,512]{1,0:T(8,128)(2,1)}, bf16[1024,512]{1,0:T(8,128)(2,1)S(1)}, u32[]{:S(2)}) %copy-start.4) | copy-done | bytes 1048600
  38.5 4.9 %shard_map.120 = (bf16[1024,512]{1,0:T(8,128)(2,1)}, bf16[1024,512]{1,0:T(8,128)(2,1)}, bf16[1024,512]{1,0:T(8,128)(2,1)}, bf16[1024,512]{1,0:T(8,128)(2,1)}, bf16[1024,512]{1,0:T(8,128)(2,1)}) custom-call(bf16[1024,512]{1,0:T(8,128)(2,1)} %copy-done, bf16[1024,512]{1,0:T(8,128)(2,1)} %copy-done.1, bf16[1024,512]{1,0:T(8,128)(2,1)} %copy-done.2, ...), custom_call_target="tpu_custom_call" | custom-call | tf_op jit(solution)/shard_map/pallas_call | solution.py:475
Async XLA Ops:
  33.6 1.0 %copy-start = (bf16[1024,512]{1,0:T(8,128)(2,1)}, bf16[1024,512]{1,0:T(8,128)(2,1)S(1)}, u32[]{:S(2)}) copy-start(bf16[1024,512]{1,0:T(8,128)(2,1)S(1)} %get-tuple-element.10.refs_0_) | copy-start | bytes 3145732
  34.5 1.0 %copy-start.1 = (bf16[1024,512]{1,0:T(8,128)(2,1)}, bf16[1024,512]{1,0:T(8,128)(2,1)S(1)}, u32[]{:S(2)}) copy-start(bf16[1024,512]{1,0:T(8,128)(2,1)S(1)} %get-tuple-element.11.refs_1_) | copy-start | bytes 3145732
  35.6 1.0 %copy-start.2 = (bf16[1024,512]{1,0:T(8,128)(2,1)}, bf16[1024,512]{1,0:T(8,128)(2,1)S(1)}, u32[]{:S(2)}) copy-start(bf16[1024,512]{1,0:T(8,128)(2,1)S(1)} %get-tuple-element.12.refs_2_) | copy-start | bytes 3145732
  36.6 1.0 %copy-start.3 = (bf16[1024,512]{1,0:T(8,128)(2,1)}, bf16[1024,512]{1,0:T(8,128)(2,1)S(1)}, u32[]{:S(2)}) copy-start(bf16[1024,512]{1,0:T(8,128)(2,1)S(1)} %get-tuple-element.13.refs_3_) | copy-start | bytes 3145732
  37.5 1.0 %copy-start.4 = (bf16[1024,512]{1,0:T(8,128)(2,1)}, bf16[1024,512]{1,0:T(8,128)(2,1)S(1)}, u32[]{:S(2)}) copy-start(bf16[1024,512]{1,0:T(8,128)(2,1)S(1)} %get-tuple-element.14.refs_4_) | copy-start | bytes 3145732

commit v6 on v5

--- a/solution.py
+++ b/solution.py
@@ -478,6 +478,7 @@
         in_specs=[vmem] * 5,
         out_specs=(anywhere,) * 5,
         scratch_shapes=[pltpu.SemaphoreType.DMA((5,))],
+        compiler_params=pltpu.CompilerParams(vmem_limit_bytes=4 * 1024 * 1024),
     )(*held)
 
 

time: 43.6 us -> 36.2 us (0.83)
  local copies, waits for them, and re-layouts: 4.93 us -> 0 us
  Pallas kernels: 37.8 us -> 35.3 us
    unnamed x10 -> x0, local copies, waits for them, and re-layouts: 4.93 us -> none
    pallas_call x1, Pallas kernels: 4.88 us -> 2.4 us  [local(): pl.pallas_call(functools.partial(write_kernel, 5), out_shape=(out,) * 5,...]
where the time goes in v6:
time: 36.2 us; the launch traced here: 36 us
  Pallas kernels  35.3 us (98%)
  between operations  0.64 us (2%)
    pallas_call x1, Pallas kernels, local(): pl.pallas_call(functools.partial(kernel, ctx_count, tp_count, heads, bloc...  32.9 us
    pallas_call x1, Pallas kernels, local(): pl.pallas_call(functools.partial(write_kernel, 5), out_shape=(out,) * 5,...  2.4 us

profile of v6, /device:TPU:0, one launch (start us, length us, event | category | flops | bytes accessed | tf_op | source)
XLA Modules:
  0.0 36.0 jit_solution(15660403788190454465)
XLA Ops:
  0.6 32.9 %shard_map.119 = (bf16[1024,512]{1,0:T(8,128)(2,1)S(1)}, bf16[1024,512]{1,0:T(8,128)(2,1)S(1)}, bf16[1024,512]{1,0:T(8,128)(2,1)S(1)}, bf16[1024,512]{1,0:T(8,128)(2,1)S(1)}, bf16[1024,512]{1,0:T(8,128)(2,1)S(1)}) custom-call(s32[6]{0:T(128)} %offs_hbm.1, bf16[1024,512]{1,0:T(8,128)(2,1)} %q_hbm.1, bf16[1024,512]{1,0:T(8,128)(2,1)} %k_hbm.1, ...), custom_call_target="tpu_custom_call" | custom-call | tf_op jit(solution)/shard_map/pallas_call | solution.py:418
  33.6 2.4 %shard_map.120 = (bf16[1024,512]{1,0:T(8,128)(2,1)}, bf16[1024,512]{1,0:T(8,128)(2,1)}, bf16[1024,512]{1,0:T(8,128)(2,1)}, bf16[1024,512]{1,0:T(8,128)(2,1)}, bf16[1024,512]{1,0:T(8,128)(2,1)}) custom-call(bf16[1024,512]{1,0:T(8,128)(2,1)S(1)} %get-tuple-element.10.refs_0_, bf16[1024,512]{1,0:T(8,128)(2,1)S(1)} %get-tuple-element.11.refs_1_, ...), custom_call_target="tpu_custom_call" | custom-call | tf_op jit(solution)/shard_map/pallas_call | solution.py:475
